TPU v7x, 128 devices: a whole 4x4x4 slice. The times are simulated.
128 devices in a mesh: dp: 8 (over z, core), head: 16 (over x, y).
Axes of the slice: x: 4, y: 4, z: 4, core: 2. Of those that a mesh axis runs over, the one named last changes fastest.
Arguments:
- tokens: bfloat16 [16, 1024, 2048], P('dp', 'head'), may hold values from -6 to 6
- cotangent: bfloat16 [16, 1024, 2048], P('dp', 'head'), may hold values from -6 to 6
- seq_lengths: int32 [16], P('dp'), may hold values from 256 to 1024, as said below
- exit_layers: int32 [16, 1024], P('dp'), may hold values from 1 to 24, as said below
- layer_index: int32 [1], replicated, may hold values from 6 to 17
- ln1_gain: float32 [2048], replicated, may hold values from 0.5 to 1.5
- ln1_shift: float32 [2048], replicated, may hold values from -4 to 4
- q_weight: float32 [2048, 2048], P('dp', 'head'), may hold values from -0.1875 to 0.1875
- q_bias: float32 [2048], replicated, may hold values from -4 to 4
- k_weight: float32 [2048, 2048], P('dp', 'head'), may hold values from -0.1875 to 0.1875
- v_weight: float32 [2048, 2048], P('dp', 'head'), may hold values from -0.125 to 0.125
- v_bias: float32 [2048], replicated, may hold values from -4 to 4
- out_weight: float32 [2048, 2048], P('dp', 'head'), may hold values from -0.5 to 0.5
- out_bias: float32 [2048], replicated, may hold values from -4 to 4
- ln2_gain: float32 [2048], replicated, may hold values from 0.5 to 1.5
- ln2_shift: float32 [2048], replicated, may hold values from -4 to 4
- up_weight: float32 [2048, 8192], P('dp', 'head'), may hold values from -0.125 to 0.125
- up_bias: float32 [8192], replicated, may hold values from -6 to 6
- down_weight: float32 [2048, 8192], P('dp', 'head'), may hold values from -0.0625 to 0.0625
- down_bias: float32 [2048], replicated, may hold values from -4 to 4
Outputs:
- result: bfloat16 [16, 1024, 2048], P('dp', 'head')
- grad_tokens: float32 [16, 1024, 2048], P('dp', 'head')
- grad_ln1_gain: float32 [2048], replicated
- grad_ln1_shift: float32 [2048], replicated
- grad_q_weight: float32 [2048, 2048], P('dp', 'head')
- grad_q_bias: float32 [2048], replicated
- grad_k_weight: float32 [2048, 2048], P('dp', 'head')
- grad_v_weight: float32 [2048, 2048], P('dp', 'head')
- grad_v_bias: float32 [2048], replicated
- grad_out_weight: float32 [2048, 2048], P('dp', 'head')
- grad_out_bias: float32 [2048], replicated
- grad_ln2_gain: float32 [2048], replicated
- grad_ln2_shift: float32 [2048], replicated
- grad_up_weight: float32 [2048, 8192], P('dp', 'head')
- grad_up_bias: float32 [8192], replicated
- grad_down_weight: float32 [2048, 8192], P('dp', 'head')
- grad_down_bias: float32 [2048], replicated
Inputs may be any that keep to these rules, and one draw needn't show every extreme that they name: `seq_lengths`: in the 2 sequences of each dp index one has 1024 tokens and exit layer 24 at every position. `exit_layers`: every other sequence's exit layers fall linearly over its own length: max(1, 24 - floor(p * r / length)) at position p, with a whole r of 12 to 23 of its own.
All inputs are finite; a program needn't handle non-finite values.
Results may differ from a plain program's by a relative error of at most 0.022.
Values may be sent and summed in bfloat16 or wider, within the bound.
No kernel may reach another device: no remote copies, remote signals or barrier semaphores. Data moves between devices by JAX's collectives and lax.ppermute only.
A program may use at most 384 MiB of HBM per device.

v0:
```python
from functools import partial

import jax
import jax.numpy as jnp
from jax import lax
from jax.experimental import pallas as pl
from jax.experimental.pallas import tpu as pltpu
from jax.sharding import Mesh
from jax.sharding import PartitionSpec as P

HEAD_DIM = 64
SPAN = 256
LOW = jnp.bfloat16
WIDE = jnp.float32
RING = 4
ROWS = ("z", "c")
COLS = ("x", "y")


def dot(left, right):
    return jnp.dot(left, right, preferred_element_type=WIDE)


def dot_t(left, right):
    return lax.dot_general(left, right, (((1,), (1,)), ((), ())), preferred_element_type=WIDE)


def dot_0(left, right):
    return lax.dot_general(left, right, (((0,), (0,)), ((), ())), preferred_element_type=WIDE)


def call(body, out_shape, grid, in_specs, out_specs, flops, traffic, scratch=(), prefetch=0, vmem=40, aliases=None):
    return pl.pallas_call(
        body,
        out_shape=out_shape,
        grid_spec=pltpu.PrefetchScalarGridSpec(
            num_scalar_prefetch=prefetch,
            grid=grid,
            in_specs=in_specs,
            out_specs=out_specs,
            scratch_shapes=list(scratch),
        ),
        compiler_params=pltpu.CompilerParams(vmem_limit_bytes=vmem * 2**20),
        input_output_aliases=aliases or {},
        cost_estimate=pl.CostEstimate(flops=flops, bytes_accessed=traffic, transcendentals=0),
    )


def whole(shape):
    return pl.BlockSpec(shape, lambda *_: (0,) * len(shape))


def struct(shape, dtype):
    return jax.ShapeDtypeStruct(shape, dtype)


def spread(array, axes, size):
    return lax.all_to_all(jnp.broadcast_to(array[None], (size,) + array.shape), axes, 0, 0)


def collect(parts, axes):
    return jnp.sum(lax.all_to_all(parts, axes, 0, 0).astype(WIDE), 0)


def swap(parts, axes):
    return lax.all_to_all(parts, axes, 0, 0)


def ring(array, step, axis="y"):
    return lax.ppermute(array, axis, [(i, (i + step) % RING) for i in range(RING)])


def ring_stack(array, axis):
    return jnp.stack([array] + [ring(array, step, axis) for step in (1, -1, 2)])


def ring_collect(parts, axis):
    came = [ring(parts[slot], step, axis) for slot, step in ((1, -1), (2, 1), (3, 2))]
    return sum(term.astype(WIDE) for term in [parts[0]] + came)


def ring_gather(rows):
    half = rows.shape[0] // 2
    first, second = rows[:half], rows[half:]
    before_first, after_second = ring(first, 1), ring(second, -1)
    before_second, after_first = ring(second, 1), ring(first, -1)
    across_first, across_second = ring(before_first, 1), ring(after_second, -1)
    return jnp.concatenate(
        [
            first, second, before_first, before_second,
            after_first, after_second, across_first, across_second,
        ],
        0,
    )


def ring_sum(rows):
    own = rows.shape[0] // RING
    half = own // 2
    start, before, after, across = (rows[i * own : (i + 1) * own] for i in range(RING))
    from_before, from_after = ring(across[:half], 1), ring(across[half:], -1)
    second_after, first_before = ring(after[half:], 1), ring(before[:half], -1)
    first_after = ring((after[:half].astype(WIDE) + from_before.astype(WIDE)).astype(LOW), 1)
    second_before = ring((before[half:].astype(WIDE) + from_after.astype(WIDE)).astype(LOW), -1)
    first = start[:half].astype(WIDE) + first_after.astype(WIDE) + first_before.astype(WIDE)
    second = start[half:].astype(WIDE) + second_after.astype(WIDE) + second_before.astype(WIDE)
    return jnp.concatenate([first, second], 0)


def tie(*arrays):
    return lax.optimization_barrier(arrays)


def gather_weight(shard):
    full = lax.all_gather(shard, ("z", "c", "x"), axis=0)
    return full.reshape((8, 4) + shard.shape)


def settle(gradient):
    return lax.psum_scatter(gradient, ROWS, scatter_dimension=0)


def qkv_body(rows_ref, weight_ref, bias_ref, out_ref):
    weight = weight_ref[...].reshape(rows_ref.shape[1], -1)
    out_ref[...] = (dot(rows_ref[...], weight) + bias_ref[...]).astype(LOW)


def qkv_project(rows, weight, bias):
    count, width = rows.shape
    zc, xs, piece, _ = weight.shape
    cols = bias.shape[-1]
    return call(
        qkv_body,
        struct((xs, count, cols), LOW),
        (xs,),
        [
            whole((count, width)),
            pl.BlockSpec((zc, None, piece, cols), lambda i: (0, i, 0, 0)),
            pl.BlockSpec((None, 1, cols), lambda i: (i, 0, 0)),
        ],
        pl.BlockSpec((None, count, cols), lambda i: (i, 0, 0)),
        2 * count * width * xs * cols,
        10 * 2**20,
        vmem=60,
    )(rows, weight, bias)


def out_body(place_ref, heads_ref, weight_ref, out_ref):
    count, _, piece, _ = weight_ref.shape
    for block in range(count):
        value = dot_t(heads_ref[0], weight_ref[block, 0])
        for x in range(1, RING):
            value += dot_t(heads_ref[x], weight_ref[block, x])
        here = slice(block * piece, (block + 1) * piece)
        store_rows(out_ref.at[:, here], place_ref, value.astype(LOW))


def store_rows(out_ref, place_ref, value):
    rows = value.shape[0] // RING
    for slot in range(RING):
        at = pl.multiple_of(place_ref[slot] * rows, rows)
        out_ref[pl.ds(at, rows)] = value[slot * rows : (slot + 1) * rows]


def out_project(places, heads, weight, at, blocks):
    xs, count, cols = heads.shape
    zc, _, piece, _ = weight.shape
    return call(
        out_body,
        struct((count, zc * piece), LOW),
        (zc // blocks,),
        [
            whole(heads.shape),
            pl.BlockSpec((blocks, xs, piece, cols), lambda i, *_: (i, 0, 0, at)),
        ],
        pl.BlockSpec((count, blocks * piece), lambda i, *_: (0, i)),
        2 * count * zc * piece * xs * cols,
        5 * 2**20,
        prefetch=1,
        vmem=60,
    )(places, heads, weight)


def heads_grad_body(rows_ref, weight_ref, out_ref):
    weight = weight_ref[...].reshape(rows_ref.shape[1], -1)
    out_ref[...] = dot(rows_ref[...], weight).astype(LOW)


def heads_grad(rows, weight, cols, at):
    count, width = rows.shape
    zc, xs, piece, _ = weight.shape
    return call(
        heads_grad_body,
        struct((xs, count, cols), LOW),
        (xs,),
        [
            whole((count, width)),
            pl.BlockSpec((zc, None, piece, cols), lambda i: (0, i, 0, at)),
        ],
        pl.BlockSpec((None, count, cols), lambda i: (i, 0, 0)),
        2 * count * width * xs * cols,
        5 * 2**20,
        vmem=60,
    )(rows, weight)


def weight_grad_body(rows_ref, grad_ref, *refs):
    out_ref = refs[-1]
    out_ref[...] = dot_0(rows_ref[...], grad_ref[...]).astype(LOW).reshape(out_ref.shape)


def weight_grads(rows, columns, total_cols, at, onto=None):
    count, width = rows.shape
    xs, _, cols = columns.shape
    piece = width // 8
    more = () if onto is None else (onto,)
    return call(
        weight_grad_body,
        struct((8, xs, piece, total_cols), LOW),
        (xs,),
        [whole((count, width)), pl.BlockSpec((None, count, cols), lambda i: (i, 0, 0))]
        + [pl.BlockSpec(memory_space=pl.ANY)] * len(more),
        pl.BlockSpec((8, None, piece, cols), lambda i: (0, i, 0, at)),
        2 * count * width * xs * cols,
        15 * 2**20,
        vmem=60,
        aliases={2: 0} if more else None,
    )(rows, columns, *more)


def add_up(total, term):
    @pl.when(pl.program_id(0) == 0)
    def _():
        total[...] = term

    @pl.when(pl.program_id(0) > 0)
    def _():
        total[...] += term


def ffn_first_body(
    place_ref, norm_ref, cot_ref, up_ref, down_ref, bias_ref,
    hidden_ref, grad_up_ref, norm_grad_ref, bias_grad_ref, total,
):
    width, cols = norm_ref.shape[1], up_ref.shape[-1]
    up_w = up_ref[...].reshape(width, cols)
    up = dot(norm_ref[...], up_w) + bias_ref[...]
    normal = 0.5 * (1.0 + lax.erf(up * 0.7071067811865476))
    hidden_ref[...] = (up * normal).astype(LOW)
    slope = normal + up * (jnp.exp(-0.5 * up * up) * 0.3989422804014327)
    grad_up = (dot(cot_ref[...], down_ref[...].reshape(width, cols)) * slope).astype(LOW)
    grad_up_ref[...] = grad_up
    bias_grad_ref[...] = jnp.sum(grad_up.astype(WIDE), 0, keepdims=True)
    add_up(total, dot_t(grad_up, up_w))

    @pl.when(pl.program_id(0) == pl.num_programs(0) - 1)
    def _():
        store_rows(norm_grad_ref, place_ref, total[...].astype(LOW))


def ffn_first(places, norm_rows, cot_rows, weight, bias):
    count, width = norm_rows.shape
    zc, xs, piece, cols = weight.shape
    size = cols // 2
    rows = whole((count, width))
    vector = pl.BlockSpec((None, 1, size), lambda i, *_: (i, 0, 0))
    wide = pl.BlockSpec((count, size), lambda i, *_: (0, i))
    return call(
        ffn_first_body,
        (
            struct((count, xs * size), LOW),
            struct((count, xs * size), LOW),
            struct((count, width), LOW),
            struct((xs, 1, size), WIDE),
        ),
        (xs,),
        [
            rows,
            rows,
            pl.BlockSpec((zc, None, piece, size), lambda i, *_: (0, i, 0, 0)),
            pl.BlockSpec((zc, None, piece, size), lambda i, *_: (0, i, 0, 1)),
            vector,
        ],
        (wide, wide, rows, vector),
        6 * count * width * xs * size,
        25 * 2**20,
        scratch=[pltpu.VMEM((count, width), WIDE)],
        prefetch=1,
        vmem=56,
    )(places, norm_rows, cot_rows, weight, weight, bias)


def ffn_second_body(
    norm_ref, cot_ref, hidden_ref, grad_up_ref, down_ref, branch_ref, weight_grad_ref, total
):
    width, cols = norm_ref.shape[1], down_ref.shape[-1]
    zc, piece, _ = weight_grad_ref.shape
    hidden = hidden_ref[...]
    weight_grad_ref[:, :, :cols] = (
        dot_0(norm_ref[...], grad_up_ref[...]).astype(LOW).reshape(zc, piece, cols)
    )
    weight_grad_ref[:, :, cols:] = dot_0(cot_ref[...], hidden).astype(LOW).reshape(zc, piece, cols)
    add_up(total, dot_t(hidden, down_ref[...].reshape(width, cols)))

    @pl.when(pl.program_id(0) == pl.num_programs(0) - 1)
    def _():
        branch_ref[...] = total[...].astype(LOW)


def ffn_second(norm_rows, cot_rows, hidden, grad_up, weight):
    count, width = norm_rows.shape
    zc, xs, piece, cols = weight.shape
    size = cols // 2
    rows = whole((count, width))
    wide = pl.BlockSpec((count, size), lambda i: (0, i))
    return call(
        ffn_second_body,
        (struct((count, width), LOW), struct(weight.shape, LOW)),
        (xs,),
        [rows, rows, wide, wide, pl.BlockSpec((zc, None, piece, size), lambda i: (0, i, 0, 1))],
        (rows, pl.BlockSpec((zc, None, piece, cols), lambda i: (0, i, 0, 0))),
        6 * count * width * xs * size,
        40 * 2**20,
        scratch=[pltpu.VMEM((count, width), WIDE)],
        vmem=56,
    )(norm_rows, cot_rows, hidden, grad_up, weight)


def only_head(array, head):
    lane = lax.broadcasted_iota(jnp.int32, array.shape, 1)
    return jnp.where(lane // HEAD_DIM == head, array, jnp.zeros_like(array))


def allowed_keys(start, extent, live_count):
    q_place = start + lax.broadcasted_iota(jnp.int32, (SPAN, extent), 0)
    k_place = lax.broadcasted_iota(jnp.int32, (SPAN, extent), 1)
    return k_place <= jnp.minimum(q_place, live_count - 1)


def slot_of(place, own):
    apart = (place - own + RING) % RING
    return jnp.where(apart == 0, 0, jnp.where(apart == RING - 1, 1, apart + 1))


def load_ordered(blocks_ref, own, into):
    rows = blocks_ref.shape[2]
    for x in range(RING):
        for y in range(RING):
            at = (x * RING + y) * rows
            into[at : at + rows] = blocks_ref[x, slot_of(y, own)]


def store_ordered(blocks_ref, x, own, cols, value):
    rows = blocks_ref.shape[2]
    for y in range(RING):
        blocks_ref[x, slot_of(y, own), :, cols] = value[y * rows : (y + 1) * rows]


def attend_body(live_ref, qkv_ref, heads_ref, exact_ref, log_ref, qkv):
    live_count = live_ref[pl.program_id(0)]
    own = live_ref[pl.num_programs(0)]
    length = exact_ref.shape[0]
    width = exact_ref.shape[1]
    load_ordered(qkv_ref, own, qkv)
    key = qkv[:, width : 2 * width]
    value = qkv[:, 2 * width :]
    for span in range(length // SPAN):
        start, extent = span * SPAN, (span + 1) * SPAN
        here = slice(start, extent)

        @pl.when(start < live_count)
        def _():
            query = qkv[here, :width]
            allowed = allowed_keys(start, extent, live_count)
            mixed, logs = [], []
            for head in range(width // HEAD_DIM):
                scores = dot_t(only_head(query, head), key[:extent]) * HEAD_DIM**-0.5
                scores = jnp.where(allowed, scores, -1e9)
                top = jnp.max(scores, 1, keepdims=True)
                terms = jnp.exp(scores - top)
                denom = jnp.sum(terms, 1, keepdims=True)
                mixed.append(dot(terms.astype(LOW), value[:extent]) / denom)
                logs.append(top + jnp.log(denom))
            lane = lax.broadcasted_iota(jnp.int32, (SPAN, width), 1)
            out = jnp.where(lane < HEAD_DIM, mixed[0], mixed[1])
            exact_ref[here] = out
            log_ref[here] = jnp.where(lane < HEAD_DIM, logs[0], logs[1])
            store_ordered(heads_ref, span, own, slice(None), out.astype(LOW))

        @pl.when(start >= live_count)
        def _():
            exact_ref[here] = jnp.zeros((SPAN, width), WIDE)
            log_ref[here] = jnp.zeros((SPAN, width), WIDE)
            heads_ref[span] = jnp.zeros(heads_ref.shape[1:], LOW)


def row_block(rows, cols):
    return pl.BlockSpec((4, 4, None, rows, cols), lambda s, *_: (0, 0, s, 0, 0))


def attend(live_counts, qkv, width):
    xs, ys, seqs, rows, _ = qkv.shape
    length = xs * ys * rows
    flat = pl.BlockSpec((None, length, width), lambda s, *_: (s, 0, 0))
    return call(
        attend_body,
        (
            struct((xs, ys, seqs, rows, width), LOW),
            struct((seqs, length, width), WIDE),
            struct((seqs, length, width), WIDE),
        ),
        (seqs,),
        [row_block(rows, 3 * width)],
        (row_block(rows, width), flat, flat),
        4 * 10**9,
        4 * 2**20,
        scratch=[pltpu.VMEM((length, 3 * width), LOW)],
        prefetch=1,
    )(live_counts, qkv)


def attend_back_body(
    live_ref, qkv_ref, grad_ref, exact_ref, log_ref, out_ref, sum_ref,
    key_total, value_total, qkv, grads,
):
    live_count = live_ref[pl.program_id(0)]
    own = live_ref[pl.num_programs(0)]
    length, width = exact_ref.shape
    factor = HEAD_DIM**-0.5
    load_ordered(qkv_ref, own, qkv)
    load_ordered(grad_ref, own, grads)
    key = qkv[:, width : 2 * width]
    value = qkv[:, 2 * width :]
    key_total[...] = jnp.zeros_like(key_total)
    value_total[...] = jnp.zeros_like(value_total)
    sum_ref[...] = jnp.zeros_like(sum_ref)
    for span in range(length // SPAN):
        start, extent = span * SPAN, (span + 1) * SPAN
        here = slice(start, extent)

        @pl.when(start < live_count)
        def _():
            query = qkv[here, :width]
            grad = grads[here]
            inner = grad.astype(WIDE) * exact_ref[here]
            logs = log_ref[here]
            allowed = allowed_keys(start, extent, live_count)
            query_total = jnp.zeros((SPAN, width), WIDE)
            for head in range(width // HEAD_DIM):
                query_h = only_head(query, head)
                grad_h = only_head(grad, head)
                log_h = logs[:, head * HEAD_DIM : head * HEAD_DIM + 1]
                row_inner = jnp.sum(only_head(inner, head), 1, keepdims=True)
                scores = dot_t(query_h, key[:extent]) * factor
                probs = jnp.exp(jnp.where(allowed, scores, -1e9) - log_h)
                d_probs = dot_t(grad_h, value[:extent])
                value_total[:extent] += dot_0(probs.astype(LOW), grad_h)
                d_scores = (probs * (d_probs - row_inner)).astype(LOW)
                query_total += dot(d_scores, only_head(key[:extent], head))
                key_total[:extent] += dot_0(d_scores, query_h)
            out = (query_total * factor).astype(LOW)
            store_ordered(out_ref, span, own, slice(0, width), out)
            sum_ref[:, :width] += jnp.sum(out.astype(WIDE), 0, keepdims=True)

        @pl.when(start >= live_count)
        def _():
            out_ref[span, :, :, :width] = jnp.zeros(out_ref.shape[1:3] + (width,), LOW)

    key_grad = (key_total[...] * factor).astype(LOW)
    value_grad = value_total[...].astype(LOW)
    for span in range(RING):
        here = slice(span * SPAN, (span + 1) * SPAN)
        store_ordered(out_ref, span, own, slice(width, 2 * width), key_grad[here])
        store_ordered(out_ref, span, own, slice(2 * width, None), value_grad[here])
    sum_ref[:, 2 * width :] = jnp.sum(value_grad.astype(WIDE), 0, keepdims=True)


def attend_back(live_counts, qkv, grads, exact, logs):
    xs, ys, seqs, rows, _ = qkv.shape
    _, length, width = exact.shape
    flat = pl.BlockSpec((None, length, width), lambda s, *_: (s, 0, 0))
    return call(
        attend_back_body,
        (struct(qkv.shape, LOW), struct((seqs, 1, 3 * width), WIDE)),
        (seqs,),
        [row_block(rows, 3 * width), row_block(rows, width), flat, flat],
        (
            row_block(rows, 3 * width),
            pl.BlockSpec((None, 1, 3 * width), lambda s, *_: (s, 0, 0)),
        ),
        8 * 10**9,
        8 * 2**20,
        scratch=[
            pltpu.VMEM((length, width), WIDE),
            pltpu.VMEM((length, width), WIDE),
            pltpu.VMEM((length, 3 * width), LOW),
            pltpu.VMEM((length, width), LOW),
        ],
        prefetch=1,
    )(live_counts, qkv, grads, exact, logs)


def norm_rows(values, gain_vec, shift_vec):
    centered = values - jnp.mean(values, -1, keepdims=True)
    inverse = lax.rsqrt(jnp.mean(centered * centered, -1, keepdims=True) + 1e-05)
    return (centered * inverse * gain_vec + shift_vec).astype(LOW)


def norm_back_body(with_low, parts_ref, rows_ref, grad_ref, gain_ref, *refs):
    gradient = parts_ref[0].astype(WIDE)
    for part in range(1, parts_ref.shape[0]):
        gradient += parts_ref[part].astype(WIDE)
    values = rows_ref[...].astype(WIDE)
    centered = values - jnp.mean(values, 1, keepdims=True)
    inverse = lax.rsqrt(jnp.mean(centered * centered, 1, keepdims=True) + 1e-05)
    unit = centered * inverse
    scaled = gradient * gain_ref[...]
    out = grad_ref[...].astype(WIDE) + inverse * (
        scaled
        - jnp.mean(scaled, 1, keepdims=True)
        - unit * jnp.mean(scaled * unit, 1, keepdims=True)
    )
    sums = [jnp.sum(gradient * unit, 0, keepdims=True), jnp.sum(gradient, 0, keepdims=True)]
    if with_low:
        keep_ref, out_ref, low_ref, sum_ref = refs
        low = (keep_ref[...] * out).astype(LOW)
        low_ref[...] = low
        sums.append(jnp.sum(low.astype(WIDE), 0, keepdims=True))
    else:
        out_ref, sum_ref = refs
    out_ref[...] = out
    sums.append(jnp.zeros((sum_ref.shape[0] - len(sums), sum_ref.shape[1]), WIDE))
    add_up(sum_ref, jnp.concatenate(sums, 0))


def norm_back(parts, rows, grad, gain, keep=None):
    count, own, width = parts.shape
    step = own // 4
    flat = pl.BlockSpec((step, width), lambda i: (i, 0))
    sums = pl.BlockSpec((8, width), lambda i: (0, 0))
    in_specs = [
        pl.BlockSpec((count, step, width), lambda i: (0, i, 0)), flat, flat,
        pl.BlockSpec((1, width), lambda i: (0, 0)),
    ]
    args = [parts, rows, grad, gain.reshape(1, width)]
    outs, specs = [struct((own, width), WIDE)], [flat]
    if keep is not None:
        in_specs.append(pl.BlockSpec((step, 1), lambda i: (i, 0)))
        args.append(keep)
        outs.append(struct((own, width), LOW))
        specs.append(flat)
    return call(
        partial(norm_back_body, keep is not None),
        tuple(outs + [struct((8, width), WIDE)]),
        (own // step,),
        in_specs,
        tuple(specs + [sums]),
        40 * own * width,
        6 * 2**20,
    )(*args)


def split_back(flat, vectors):
    pieces, start = [], 0
    for v in vectors:
        pieces.append(flat[start : start + v.size])
        start += v.size
    return pieces


def last_totals(vectors, columns, ready):
    shared = jnp.concatenate([v.reshape(-1, 128) for v in vectors], 0)
    rows, more = shared.shape[0], columns.shape[0]
    parts = spread(jnp.concatenate([shared, columns, ready], 0), COLS, 16)
    part = jnp.sum(parts[:, :rows], 0)
    part = jnp.concatenate([part, parts[:, rows : rows + more].reshape(-1, 128)], 0)
    part = jnp.sum(spread(part, ROWS, 8), 0)
    placed = part[rows:].reshape(16, more, 128)
    totals = split_back(part[:rows].reshape(-1), vectors)
    totals += [placed[:, i].reshape(-1) for i in range(more)]
    return totals, parts[:, rows + more :]


def shards(
    tokens, cotangent, seq_lengths, exit_layers, layer_index,
    ln1_gain, ln1_shift, q_weight, q_bias, k_weight, v_weight, v_bias, out_weight, out_bias,
    ln2_gain, ln2_shift, up_weight, up_bias, down_weight, down_bias,
):
    seqs, own_rows, width = tokens.shape
    own = seqs * own_rows
    full_len = exit_layers.shape[1]
    x_at, y_at = lax.axis_index("x"), lax.axis_index("y")
    head_at = x_at * RING + y_at
    head_cols = q_weight.shape[1]
    ff_cols = up_weight.shape[1]

    positions = jnp.arange(full_len)
    live_all = (positions[None, :] < seq_lengths[:, None]) & (exit_layers > layer_index[0])
    live_counts = jnp.concatenate(
        [jnp.sum(live_all.astype(jnp.int32), 1), y_at.astype(jnp.int32).reshape(1)]
    )
    slots = jnp.arange(RING, dtype=jnp.int32)
    apart = jnp.array([0, RING - 1, 1, 2], jnp.int32)
    places = (y_at.astype(jnp.int32) + apart) % RING
    x_places = (x_at.astype(jnp.int32) + apart) % RING
    live_mine = lax.dynamic_slice_in_dim(live_all, head_at * own_rows, own_rows, 1)
    keep = live_mine.reshape(-1, 1).astype(WIDE)

    w_attn = gather_weight(
        jnp.concatenate([q_weight, k_weight, v_weight, out_weight], 1).astype(LOW)
    )
    w_ff = jnp.concatenate([up_weight, down_weight], 1).astype(LOW)

    inputs = tokens.astype(WIDE).reshape(own, width)
    norm1 = ring_gather(norm_rows(inputs, ln1_gain, ln1_shift))
    flat_cot = cotangent.reshape(own, width)
    g_ffn = (keep * flat_cot.astype(WIDE)).astype(LOW)
    norm1, w_ff = tie(norm1, ring_stack(w_ff, "x"))
    w_ff = lax.all_gather(w_ff, ROWS, axis=0)

    def mine(vector, cols):
        return lax.dynamic_index_in_dim(vector.reshape(RING, RING, cols), y_at, 1, False)

    bias = jnp.concatenate(
        [mine(q_bias, head_cols), jnp.zeros((RING, head_cols), WIDE), mine(v_bias, head_cols)], 1
    ).reshape(RING, 1, 3 * head_cols)
    qkv = qkv_project(norm1, w_attn, bias)
    rows5 = (RING, RING, seqs, own_rows)
    qkv, g_ffn = tie(qkv, g_ffn)
    cot_rows = ring_gather(g_ffn)
    qkv = swap(qkv, "x").reshape(rows5 + (3 * head_cols,))
    heads, exact, logs = attend(live_counts, qkv, head_cols)
    heads, cot_rows = tie(heads, cot_rows)
    heads = swap(heads.reshape(RING, RING * own, head_cols), "x")
    branch1 = ring_sum(out_project(slots, heads, w_attn, 3, 4)) + out_bias
    middle = inputs + keep * branch1
    norm2 = ring_gather(norm_rows(middle, ln2_gain, ln2_shift))

    ff_bias = mine(up_bias, ff_cols)[x_places].reshape(RING, 1, ff_cols)
    hidden, grad_up, g_norm2, up_bias_part = ffn_first(places, norm2, cot_rows, w_ff, ff_bias)
    g_norm2 = swap(g_norm2.reshape(RING, own, width), "y")
    g_norm2, branch2, ff_grad = tie(
        g_norm2, *ffn_second(norm2, cot_rows, hidden, grad_up, w_ff)
    )
    ff_grad = settle(ff_grad)
    grad_mid, g_attn, sums2 = norm_back(g_norm2, middle, flat_cot, ln2_gain, keep)
    attn_rows = ring_gather(g_attn)
    g_heads = heads_grad(attn_rows, w_attn, head_cols, 3)
    g_heads, branch2 = tie(swap(g_heads, "x").reshape(rows5 + (head_cols,)), branch2)
    branch2 = ring_collect(branch2.reshape(RING, own, width), "y") + down_bias
    result = (middle + keep * branch2).astype(LOW).reshape(tokens.shape)
    d_qkv, d_sums = attend_back(live_counts, qkv, g_heads, exact, logs)
    d_qkv, attn_rows = tie(d_qkv, attn_rows)
    attn_grad = weight_grads(attn_rows, heads, 4 * head_cols, 3)
    d_qkv = swap(d_qkv.reshape(RING, RING * own, 3 * head_cols), "x")

    up_bias_full = jnp.zeros((RING, RING, ff_cols), WIDE)
    for slot in range(RING):
        up_bias_full = lax.dynamic_update_slice(
            up_bias_full, up_bias_part[slot][None], (x_places[slot], y_at, 0)
        )
    early = (
        sums2[2],
        sums2[0],
        sums2[1],
        up_bias_full,
        jnp.sum(g_ffn.astype(WIDE), 0),
    )
    early_flat = jnp.concatenate([v.reshape(-1) for v in early]).reshape(16, -1, 128)
    d_qkv, attn_grad, result, early_flat = tie(d_qkv, attn_grad, result, early_flat)
    part = collect(early_flat, COLS)
    attn_grad = weight_grads(norm1, d_qkv, 4 * head_cols, 0, attn_grad)
    d_qkv, attn_grad, part, ff_grad = tie(d_qkv, attn_grad, part, ff_grad)
    attn_grad = settle(attn_grad)
    part = jnp.sum(spread(part, ROWS, 8), 0)
    g_norm1 = out_project(places, d_qkv, w_attn, 0, 2)
    g_norm1, part = tie(g_norm1, part)
    ff_grad = ring_collect(ff_grad, "x")
    g_norm1 = swap(g_norm1.reshape(RING, own, width), "y")
    g_norm1, attn_grad = tie(g_norm1, attn_grad)
    here = [lax.dynamic_index_in_dim(attn_grad, x_places[i], 0, False) for i in range(RING)]
    attn_grad = ring_collect(here, "x")
    grad_tokens, sums1 = norm_back(g_norm1, tokens.reshape(own, width), grad_mid, ln1_gain)
    grad_tokens = grad_tokens.reshape(tokens.shape)
    d_sums = jnp.sum(d_sums, 0).reshape(3, head_cols)
    ln1_totals, early_totals = last_totals((sums1[0], sums1[1]), d_sums[::2], part)
    ln1_gain_sum, ln1_shift_sum, q_bias_sum, v_bias_sum = ln1_totals
    out_bias_sum, ln2_gain_sum, ln2_shift_sum, up_bias_sum, down_bias_sum = split_back(
        early_totals.reshape(-1), early
    )
    return (
        result,
        grad_tokens,
        ln1_gain_sum,
        ln1_shift_sum,
        attn_grad[:, :head_cols],
        q_bias_sum,
        attn_grad[:, head_cols : 2 * head_cols],
        attn_grad[:, 2 * head_cols : 3 * head_cols],
        v_bias_sum,
        attn_grad[:, 3 * head_cols :],
        out_bias_sum,
        ln2_gain_sum,
        ln2_shift_sum,
        ff_grad[:, :ff_cols],
        up_bias_sum,
        ff_grad[:, ff_cols:],
        down_bias_sum,
    )


def solution(mesh):
    wide = Mesh(mesh.devices.reshape(4, 2, 4, 4), ("z", "c", "x", "y"))
    act = P(ROWS, COLS, None)
    weight = P(ROWS, COLS)
    vector = P()
    in_specs = (
        act, act, P(ROWS), P(ROWS, None), vector, vector, vector,
        weight, vector, weight, weight, vector, weight, vector, vector, vector,
        weight, vector, weight, vector,
    )
    out_specs = (
        act, act, vector, vector, weight, vector, weight, weight, vector, weight,
        vector, vector, vector, weight, vector, weight, vector,
    )
    return jax.shard_map(
        shards, mesh=wide, in_specs=in_specs, out_specs=out_specs, check_vma=False
    )
```

profile of v0, /device:TPU:1, one launch (start us, length us, event | category | flops | bytes accessed | tf_op | source)
XLA Modules:
  0.0 437.7 jit_solution(2621669230841588497)
XLA Ops:
  11.3 3.7 collective-permute-start.8
  16.8 2.8 collective-permute-start.3
  19.7 13.0 %collective-permute-done = bf16[64,2048]{1,0:T(8,128)(2,1)S(1)} collective-permute-done((bf16[64,2048]{1,0:T(8,128)(2,1)S(1)}, bf16[64,2048]{1,0:T(8,128)(2,1)S(1)}, u32[]{:S(2)}, u32[]{:S(2)}) %collective-permute-start) | collective-permute-done | bytes 262176 | tf_op jit(solution)/shard_map/ppermute | solution.py:70
  35.0 3.3 collective-permute-done.2
  40.3 3.7 collective-permute-done.5
  44.0 2.9 collective-permute-done.6
  51.2 19.5 %all-gather.4.cloned.1.call-done = bf16[32,256,512]{2,1,0:T(8,128)(2,1)} async-done(((bf16[1,256,512]{2,1,0:T(8,128)(2,1)}), bf16[32,256,512]{2,1,0:T(8,128)(2,1)}) %all-gather.4.cloned.1.call-update) | async-done | bytes 8388624 | tf_op jit(solution)/shard_map/all_gather | solution.py:115
  70.7 8.3 %shard_map.332 = bf16[4,512,384]{2,1,0:T(8,128)(2,1)} custom-call(bf16[512,2048]{1,0:T(8,128)(2,1)} %copy-done.10, bf16[8,4,256,512]{3,2,1,0:T(8,128)(2,1)} %bitcast.109, f32[4,1,384]{2,1,0:T(1,128)} %reshape.336.bias_ref), custom_call_target="tpu_custom_call" | custom-call | flops 3221225472 | bytes 10485760 | tf_op jit(solution)/shard_map/pallas_call | solution.py:132
  79.1 2.5 collective-permute-start.12
  81.9 2.5 collective-permute-start.11
  85.2 4.4 %all-to-all-start = ((bf16[4,512,384]{2,1,0:T(8,128)(2,1)}), bf16[4,512,384]{2,1,0:T(8,128)(2,1)}, u32[]{:S(2)}, u32[]{:S(2)}) async-start(bf16[4,512,384]{2,1,0:T(8,128)(2,1)} %shard_map.332), calls=%async_computation | async-start | bytes 3145728 | tf_op jit(solution)/shard_map/all_to_all | solution.py:66
  92.1 3.8 collective-permute-done.10
  98.0 3.4 collective-permute-done.13
  102.9 6.5 %all-to-all-done = bf16[4,512,384]{2,1,0:T(8,128)(2,1)} async-done(((bf16[4,512,384]{2,1,0:T(8,128)(2,1)}), bf16[4,512,384]{2,1,0:T(8,128)(2,1)}, u32[]{:S(2)}, u32[]{:S(2)}) %all-to-all-start) | async-done | bytes 1572896 | tf_op jit(solution)/shard_map/all_to_all | solution.py:66
  109.4 6.9 %shard_map.333 = (bf16[4,4,2,64,128]{4,3,2,1,0:T(8,128)(2,1)S(1)}, f32[2,1024,128]{2,1,0:T(8,128)S(1)}, f32[2,1024,128]{2,1,0:T(8,128)S(1)}) custom-call(s32[3]{0:T(128)S(1)} %pad_add_fusion.live_ref, bf16[4,4,2,64,384]{4,3,2,1,0:T(8,128)(2,1)} %bitcast.18.qkv_ref), custom_call_target="tpu_custom_call" | custom-call | flops 4000000000 | bytes 4194304 | tf_op jit(solution)/shard_map/pallas_call | solution.py:405
  116.3 10.0 %all_to_all.50.heads_ref.grad_ref = bf16[4,512,128]{2,1,0:T(8,128)(2,1)} all-to-all(bf16[4,512,128]{2,1,0:T(8,128)(2,1)S(1)} %bitcast.106), channel_id=1, replica_groups=mesh['z'=4,'c'=2,'x'=4,'y'=4] {'x'}, dimensions={0} | all-to-all | bytes 1048576 | tf_op jit(solution)/shard_map/all_to_all | solution.py:66
  126.9 5.8 %shard_map.334 = bf16[512,2048]{1,0:T(8,128)(2,1)} custom-call(s32[4]{0:T(128)} %iota.7.place_ref, bf16[4,512,128]{2,1,0:T(8,128)(2,1)} %all_to_all.50.heads_ref.grad_ref, bf16[8,4,256,512]{3,2,1,0:T(8,128)(2,1)} %bitcast.110), custom_call_target="tpu_custom_call" | custom-call | flops 1073741824 | bytes 5242880 | tf_op jit(solution)/shard_map/pallas_call | solution.py:168
  134.2 2.7 collective-permute-start.19
  136.9 4.1 collective-permute-done.15
  143.1 5.9 %collective-permute-done.16 = bf16[64,2048]{1,0:T(8,128)(2,1)S(1)} collective-permute-done((bf16[64,2048]{1,0:T(8,128)(2,1)S(1)}, bf16[64,2048]{1,0:T(8,128)(2,1)S(1)}, u32[]{:S(2)}, u32[]{:S(2)}) %collective-permute-start.16) | collective-permute-done | bytes 262176 | tf_op jit(solution)/shard_map/ppermute | solution.py:70
  151.8 3.0 collective-permute-done.20
  160.7 2.6 collective-permute-start.23
  170.1 3.7 collective-permute-done.25
  175.3 21.5 %shard_map.335 = (bf16[512,2048]{1,0:T(8,128)(2,1)}, bf16[512,2048]{1,0:T(8,128)(2,1)}, bf16[512,2048]{1,0:T(8,128)(2,1)}, f32[4,1,512]{2,1,0:T(1,128)}) custom-call(s32[4]{0:T(128)} %get-tuple-element.157.place_ref, bf16[512,2048]{1,0:T(8,128)(2,1)} %constant_dynamic-update-slice_fusion.14.norm_ref, ...), custom_call_target="tpu_custom_call" | custom-call | flops 12884901888 | bytes 26214400 | tf_op jit(solution)/shard_map/pallas_call | solution.py:268
  196.8 4.5 %all-to-all-start.2 = ((bf16[4,128,2048]{2,1,0:T(8,128)(2,1)}), bf16[4,128,2048]{2,1,0:T(8,128)(2,1)}, u32[]{:S(2)}, u32[]{:S(2)}) async-start(bf16[4,128,2048]{2,1,0:T(8,128)(2,1)} %bitcast.118), calls=%async_computation.2 | async-start | bytes 4194304 | tf_op jit(solution)/shard_map/all_to_all | solution.py:66
  201.3 21.5 %shard_map.336 = (bf16[512,2048]{1,0:T(8,128)(2,1)}, bf16[8,4,256,1024]{3,2,1,0:T(8,128)(2,1)}) custom-call(bf16[512,2048]{1,0:T(8,128)(2,1)} %constant_dynamic-update-slice_fusion.14.norm_ref, bf16[512,2048]{1,0:T(8,128)(2,1)} %constant_dynamic-update-slice_fusion.7.cot_ref, bf16[512,2048]{1,0:T(8,128)(2,1)} %get-tuple-element.66.hidden_ref, ...), custom_call_target="tpu_custom_call" | custom-call | flops 12884901888 | bytes 41943040 | tf_op jit(solution)/shard_map/pallas_call | solution.py:316
  231.5 3.5 shard_map.337
  236.0 2.6 collective-permute-start.30
  253.8 5.9 %shard_map.338 = bf16[4,512,128]{2,1,0:T(8,128)(2,1)} custom-call(bf16[512,2048]{1,0:T(8,128)(2,1)} %constant_dynamic-update-slice_fusion.21.rows_ref, bf16[8,4,256,512]{3,2,1,0:T(8,128)(2,1)} %bitcast.111), custom_call_target="tpu_custom_call" | custom-call | flops 1073741824 | bytes 5242880 | tf_op jit(solution)/shard_map/pallas_call | solution.py:192
  259.6 3.9 all-to-all-start.3
  264.2 6.3 %all-to-all-done.3 = bf16[4,512,128]{2,1,0:T(8,128)(2,1)S(1)} async-done(((bf16[4,512,128]{2,1,0:T(8,128)(2,1)}), bf16[4,512,128]{2,1,0:T(8,128)(2,1)S(1)}, u32[]{:S(2)}, u32[]{:S(2)}) %all-to-all-start.3) | async-done | bytes 524320 | tf_op jit(solution)/shard_map/all_to_all | solution.py:66
  272.9 10.5 %shard_map.339 = (bf16[4,4,2,64,384]{4,3,2,1,0:T(8,128)(2,1)}, f32[2,1,384]{2,1,0:T(1,128)S(1)}) custom-call(s32[3]{0:T(128)S(1)} %pad_add_fusion.live_ref, bf16[4,4,2,64,384]{4,3,2,1,0:T(8,128)(2,1)} %bitcast.18.qkv_ref, bf16[4,4,2,64,128]{4,3,2,1,0:T(8,128)(2,1)S(1)} %bitcast.105, f32[2,1024,128]{2,1,0:T(8,128)S(1)} %copy-done.7, f32[2,1024,128]{2,1,0:T(8,128)S(1)} %copy-done.9), custom_call_target="tpu_custom_call" | custom-call | flops 8000000000 | bytes 8388608 | tf_op jit(solution)/shard_map/pallas_call | solution.py:482
  283.4 4.4 %all-to-all-start.4 = ((bf16[4,512,384]{2,1,0:T(8,128)(2,1)}), bf16[4,512,384]{2,1,0:T(8,128)(2,1)}, u32[]{:S(2)}, u32[]{:S(2)}) async-start(bf16[4,512,384]{2,1,0:T(8,128)(2,1)} %bitcast.25), calls=%async_computation.4 | async-start | bytes 3145728 | tf_op jit(solution)/shard_map/all_to_all | solution.py:66
  294.0 6.1 %shard_map.340.refs_0_ = bf16[8,4,256,512]{3,2,1,0:T(8,128)(2,1)} custom-call(bf16[512,2048]{1,0:T(8,128)(2,1)} %constant_dynamic-update-slice_fusion.21.rows_ref, bf16[4,512,128]{2,1,0:T(8,128)(2,1)} %all_to_all.50.heads_ref.grad_ref), custom_call_target="tpu_custom_call" | custom-call | flops 1073741824 | bytes 15728640 | tf_op jit(solution)/shard_map/pallas_call | solution.py:217
  300.2 5.6 %collective-permute-done.34 = bf16[128,2048]{1,0:T(8,128)(2,1)} collective-permute-done((bf16[128,2048]{1,0:T(8,128)(2,1)S(1)}, bf16[128,2048]{1,0:T(8,128)(2,1)}, u32[]{:S(2)}, u32[]{:S(2)}) %collective-permute-start.34) | collective-permute-done | bytes 524320 | tf_op jit(solution)/shard_map/ppermute | solution.py:70
  308.2 4.7 %all-to-all-start.5 = ((f32[16,8,128]{2,1,0:T(8,128)}), f32[16,8,128]{2,1,0:T(8,128)S(1)}, u32[]{:S(2)}, u32[]{:S(2)}) async-start(f32[16,8,128]{2,1,0:T(8,128)} %bitcast.34), calls=%async_computation.5 | async-start | bytes 131072 | tf_op jit(solution)/shard_map/all_to_all | solution.py:62
  312.9 8.3 %shard_map.341 = bf16[8,4,256,512]{3,2,1,0:T(8,128)(2,1)} custom-call(bf16[512,2048]{1,0:T(8,128)(2,1)} %copy-done.10, bf16[4,512,384]{2,1,0:T(8,128)(2,1)} %all-to-all-done.4.grad_ref.heads_ref, bf16[8,4,256,512]{3,2,1,0:T(8,128)(2,1)} %shard_map.340.refs_0_), custom_call_target="tpu_custom_call", output_to_operand_aliasing={{}: (2, {})} | custom-call | flops 3221225472 | bytes 15728640 | tf_op jit(solution)/shard_map/pallas_call | solution.py:217
  323.8 20.5 %all-to-all-start.6 = ((f32[8,8,128]{2,1,0:T(8,128)}), f32[8,8,128]{2,1,0:T(8,128)S(1)}, u32[]{:S(2)}, u32[]{:S(2)}) async-start(f32[8,8,128]{2,1,0:T(8,128)} %broadcast_in_dim.20), calls=%async_computation.7 | async-start | bytes 65536 | tf_op jit(solution)/shard_map/all_to_all | solution.py:58
  344.3 9.3 %shard_map.342 = bf16[512,2048]{1,0:T(8,128)(2,1)} custom-call(s32[4]{0:T(128)} %get-tuple-element.157.place_ref, bf16[4,512,384]{2,1,0:T(8,128)(2,1)} %all-to-all-done.4.grad_ref.heads_ref, bf16[8,4,256,512]{3,2,1,0:T(8,128)(2,1)} %bitcast.112), custom_call_target="tpu_custom_call" | custom-call | flops 3221225472 | bytes 5242880 | tf_op jit(solution)/shard_map/pallas_call | solution.py:168
  353.6 4.5 %all-to-all-start.7 = ((bf16[4,128,2048]{2,1,0:T(8,128)(2,1)}), bf16[4,128,2048]{2,1,0:T(8,128)(2,1)S(1)}, u32[]{:S(2)}, u32[]{:S(2)}) async-start(bf16[4,128,2048]{2,1,0:T(8,128)(2,1)} %bitcast.115), calls=%async_computation.8 | async-start | bytes 4194304 | tf_op jit(solution)/shard_map/all_to_all | solution.py:66
  358.0 2.6 slice_bitcast_fusion.2
  364.4 21.2 %collective-permute-done.39 = bf16[256,1024]{1,0:T(8,128)(2,1)S(1)} collective-permute-done((bf16[256,1024]{1,0:T(8,128)(2,1)}, bf16[256,1024]{1,0:T(8,128)(2,1)S(1)}, u32[]{:S(2)}, u32[]{:S(2)}) %collective-permute-start.39) | collective-permute-done | bytes 524320 | tf_op jit(solution)/shard_map/ppermute | solution.py:70
  385.6 4.3 collective-permute-done.40
  397.2 2.7 shard_map.343
  400.7 5.9 %all-to-all-start.8 = ((f32[16,42,128]{2,1,0:T(8,128)}), f32[16,42,128]{2,1,0:T(8,128)S(1)}, u32[]{:S(2)}, u32[]{:S(2)}) async-start(f32[16,42,128]{2,1,0:T(8,128)} %broadcast_in_dim.22), calls=%async_computation.10 | async-start | bytes 786432 | tf_op jit(solution)/shard_map/all_to_all | solution.py:58
  406.6 4.9 %collective-permute-done.37 = bf16[256,512]{1,0:T(8,128)(2,1)} collective-permute-done((bf16[256,512]{1,0:T(8,128)(2,1)S(1)}, bf16[256,512]{1,0:T(8,128)(2,1)}, u32[]{:S(2)}, u32[]{:S(2)}) %collective-permute-start.37) | collective-permute-done | bytes 262176 | tf_op jit(solution)/shard_map/ppermute | solution.py:70
  416.6 6.6 %all-to-all-start.9 = ((f32[8,64,128]{2,1,0:T(8,128)}), f32[8,64,128]{2,1,0:T(8,128)S(1)}, u32[]{:S(2)}, u32[]{:S(2)}) async-start(f32[8,64,128]{2,1,0:T(8,128)} %broadcast_in_dim.23), calls=%async_computation.11 | async-start | bytes 524288 | tf_op jit(solution)/shard_map/all_to_all | solution.py:58
  424.4 5.3 %all-to-all-done.9 = f32[8,64,128]{2,1,0:T(8,128)S(1)} async-done(((f32[8,64,128]{2,1,0:T(8,128)}), f32[8,64,128]{2,1,0:T(8,128)S(1)}, u32[]{:S(2)}, u32[]{:S(2)}) %all-to-all-start.9) | async-done | bytes 262176 | tf_op jit(solution)/shard_map/all_to_all | solution.py:58
  (247 shorter events, 92.5 us)
Async XLA Ops:
  7.2 63.5 %all-gather.4.cloned.1.call-start = ((), (), s32[]{:S(2)}) async-start(), calls=%async_computation.12 | async-start | bytes 8650752 | tf_op jit(solution)/shard_map/all_gather | solution.py:115
  10.1 165.2 %all-gather.6.cloned.1.call-start = ((), (), s32[]{:S(2)}) async-start(), calls=%async_computation.15 | async-start | bytes 18874368 | tf_op jit(solution)/shard_map/all_gather | solution.py:619
  11.3 32.7 %collective-permute-start.8 = (bf16[256,1024]{1,0:T(8,128)(2,1)S(1)}, bf16[256,1024]{1,0:T(8,128)(2,1)S(1)}, u32[]{:S(2)}, u32[]{:S(2)}) collective-permute-start(bf16[256,1024]{1,0:T(8,128)(2,1)S(1)} %pad_maximum_fusion.2), channel_id=1, source_target_pairs={{0,8},{4,12},{8,0},{12,4},{1,9},{5,13},{9,1},{13,5},{2,10},{6,14},... | collective-permute-start | bytes 1572872 | tf_op jit(solution)/shard_map/ppermute | solution.py:70
  15.0 29.0 %collective-permute-start.7 = (bf16[256,1024]{1,0:T(8,128)(2,1)S(1)}, bf16[256,1024]{1,0:T(8,128)(2,1)S(1)}, u32[]{:S(2)}, u32[]{:S(2)}) collective-permute-start(bf16[256,1024]{1,0:T(8,128)(2,1)S(1)} %pad_maximum_fusion.2), channel_id=1, source_target_pairs={{0,12},{4,0},{8,4},{12,8},{1,13},{5,1},{9,5},{13,9},{2,14},{6,2},{... | collective-permute-start | bytes 1572872 | tf_op jit(solution)/shard_map/ppermute | solution.py:70
  16.8 16.6 %collective-permute-start.3 = (bf16[64,2048]{1,0:T(8,128)(2,1)S(1)}, bf16[64,2048]{1,0:T(8,128)(2,1)S(1)}, u32[]{:S(2)}, u32[]{:S(2)}) collective-permute-start(bf16[64,2048]{1,0:T(8,128)(2,1)S(1)} %get-tuple-element.134), channel_id=1, source_target_pairs={{0,3},{1,0},{2,1},{3,2},{4,7},{5,4},{6,5},{7,6},{8,11},{9,8},{10,9... | collective-permute-start | bytes 786440 | tf_op jit(solution)/shard_map/ppermute | solution.py:70
  19.6 13.1 %collective-permute-start.1 = (bf16[64,2048]{1,0:T(8,128)(2,1)S(1)}, bf16[64,2048]{1,0:T(8,128)(2,1)S(1)}, u32[]{:S(2)}, u32[]{:S(2)}) collective-permute-start(bf16[64,2048]{1,0:T(8,128)(2,1)S(1)} %get-tuple-element.134), channel_id=1, source_target_pairs={{0,1},{1,2},{2,3},{3,0},{4,5},{5,6},{6,7},{7,4},{8,9},{9,10},{10,1... | collective-permute-start | bytes 786440 | tf_op jit(solution)/shard_map/ppermute | solution.py:70
  19.6 13.1 %collective-permute-start = (bf16[64,2048]{1,0:T(8,128)(2,1)S(1)}, bf16[64,2048]{1,0:T(8,128)(2,1)S(1)}, u32[]{:S(2)}, u32[]{:S(2)}) collective-permute-start(bf16[64,2048]{1,0:T(8,128)(2,1)S(1)} %get-tuple-element.135), channel_id=1, source_target_pairs={{0,1},{1,2},{2,3},{3,0},{4,5},{5,6},{6,7},{7,4},{8,9},{9,10},{10,1... | collective-permute-start | bytes 786440 | tf_op jit(solution)/shard_map/ppermute | solution.py:70
  32.8 14.2 %collective-permute-start.6 = (bf16[256,1024]{1,0:T(8,128)(2,1)S(1)}, bf16[256,1024]{1,0:T(8,128)(2,1)S(1)}, u32[]{:S(2)}, u32[]{:S(2)}) collective-permute-start(bf16[256,1024]{1,0:T(8,128)(2,1)S(1)} %pad_maximum_fusion.2), channel_id=1, source_target_pairs={{0,4},{4,8},{8,12},{12,0},{1,5},{5,9},{9,13},{13,1},{2,6},{6,10},{... | collective-permute-start | bytes 1572872 | tf_op jit(solution)/shard_map/ppermute | solution.py:70
  79.1 10.6 %collective-permute-start.12 = (bf16[64,2048]{1,0:T(8,128)(2,1)S(1)}, bf16[64,2048]{1,0:T(8,128)(2,1)S(1)}, u32[]{:S(2)}, u32[]{:S(2)}) collective-permute-start(bf16[64,2048]{1,0:T(8,128)(2,1)S(1)} %get-tuple-element.132), channel_id=1, source_target_pairs={{0,3},{1,0},{2,1},{3,2},{4,7},{5,4},{6,5},{7,6},{8,11},{9,8},{10,9... | collective-permute-start | bytes 786440 | tf_op jit(solution)/shard_map/ppermute | solution.py:70
  81.6 9.5 %collective-permute-start.9 = (bf16[64,2048]{1,0:T(8,128)(2,1)S(1)}, bf16[64,2048]{1,0:T(8,128)(2,1)S(1)}, u32[]{:S(2)}, u32[]{:S(2)}) collective-permute-start(bf16[64,2048]{1,0:T(8,128)(2,1)S(1)} %get-tuple-element.133), channel_id=1, source_target_pairs={{0,1},{1,2},{2,3},{3,0},{4,5},{5,6},{6,7},{7,4},{8,9},{9,10},{10,1... | collective-permute-start | bytes 786440 | tf_op jit(solution)/shard_map/ppermute | solution.py:70
  81.7 14.2 %collective-permute-start.10 = (bf16[64,2048]{1,0:T(8,128)(2,1)S(1)}, bf16[64,2048]{1,0:T(8,128)(2,1)S(1)}, u32[]{:S(2)}, u32[]{:S(2)}) collective-permute-start(bf16[64,2048]{1,0:T(8,128)(2,1)S(1)} %get-tuple-element.132), channel_id=1, source_target_pairs={{0,1},{1,2},{2,3},{3,0},{4,5},{5,6},{6,7},{7,4},{8,9},{9,10},{10,1... | collective-permute-start | bytes 786440 | tf_op jit(solution)/shard_map/ppermute | solution.py:70
  81.9 14.7 %collective-permute-start.11 = (bf16[64,2048]{1,0:T(8,128)(2,1)S(1)}, bf16[64,2048]{1,0:T(8,128)(2,1)S(1)}, u32[]{:S(2)}, u32[]{:S(2)}) collective-permute-start(bf16[64,2048]{1,0:T(8,128)(2,1)S(1)} %get-tuple-element.133), channel_id=1, source_target_pairs={{0,3},{1,0},{2,1},{3,2},{4,7},{5,4},{6,5},{7,6},{8,11},{9,8},{10,9... | collective-permute-start | bytes 786440 | tf_op jit(solution)/shard_map/ppermute | solution.py:70
  85.2 24.1 %all-to-all-start = ((bf16[4,512,384]{2,1,0:T(8,128)(2,1)}), bf16[4,512,384]{2,1,0:T(8,128)(2,1)}, u32[]{:S(2)}, u32[]{:S(2)}) async-start(bf16[4,512,384]{2,1,0:T(8,128)(2,1)} %shard_map.332), calls=%async_computation | async-start | bytes 3145728 | tf_op jit(solution)/shard_map/all_to_all | solution.py:66
  89.7 12.5 %collective-permute-start.14 = (bf16[64,2048]{1,0:T(8,128)(2,1)S(1)}, bf16[64,2048]{1,0:T(8,128)(2,1)S(1)}, u32[]{:S(2)}, u32[]{:S(2)}) collective-permute-start(bf16[64,2048]{1,0:T(8,128)(2,1)S(1)} %collective-permute-done.12), channel_id=1, source_target_pairs={{0,3},{1,0},{2,1},{3,2},{4,7},{5,4},{6,5},{7,6},{8,11},{9,8},{10,9... | collective-permute-start | bytes 786440 | tf_op jit(solution)/shard_map/ppermute | solution.py:70
  91.1 10.4 %collective-permute-start.13 = (bf16[64,2048]{1,0:T(8,128)(2,1)S(1)}, bf16[64,2048]{1,0:T(8,128)(2,1)S(1)}, u32[]{:S(2)}, u32[]{:S(2)}) collective-permute-start(bf16[64,2048]{1,0:T(8,128)(2,1)S(1)} %collective-permute-done.9), channel_id=1, source_target_pairs={{0,1},{1,2},{2,3},{3,0},{4,5},{5,6},{6,7},{7,4},{8,9},{9,10},{10,1... | collective-permute-start | bytes 786440 | tf_op jit(solution)/shard_map/ppermute | solution.py:70
  134.1 6.9 %collective-permute-start.15 = (bf16[64,2048]{1,0:T(8,128)(2,1)S(1)}, bf16[64,2048]{1,0:T(8,128)(2,1)S(1)}, u32[]{:S(2)}, u32[]{:S(2)}) collective-permute-start(bf16[64,2048]{1,0:T(8,128)(2,1)S(1)} %get-tuple-element.113), channel_id=1, source_target_pairs={{0,1},{1,2},{2,3},{3,0},{4,5},{5,6},{6,7},{7,4},{8,9},{9,10},{10,1... | collective-permute-start | bytes 786440 | tf_op jit(solution)/shard_map/ppermute | solution.py:70
  134.2 7.1 %collective-permute-start.19 = (bf16[64,2048]{1,0:T(8,128)(2,1)S(1)}, bf16[64,2048]{1,0:T(8,128)(2,1)S(1)}, u32[]{:S(2)}, u32[]{:S(2)}) collective-permute-start(bf16[64,2048]{1,0:T(8,128)(2,1)S(1)} %get-tuple-element.114), channel_id=1, source_target_pairs={{0,3},{1,0},{2,1},{3,2},{4,7},{5,4},{6,5},{7,6},{8,11},{9,8},{10,9... | collective-permute-start | bytes 786440 | tf_op jit(solution)/shard_map/ppermute | solution.py:70
  141.1 7.9 %collective-permute-start.16 = (bf16[64,2048]{1,0:T(8,128)(2,1)S(1)}, bf16[64,2048]{1,0:T(8,128)(2,1)S(1)}, u32[]{:S(2)}, u32[]{:S(2)}) collective-permute-start(bf16[64,2048]{1,0:T(8,128)(2,1)S(1)} %add_convert_fusion.3), channel_id=1, source_target_pairs={{0,1},{1,2},{2,3},{3,0},{4,5},{5,6},{6,7},{7,4},{8,9},{9,10},{10,1... | collective-permute-start | bytes 786440 | tf_op jit(solution)/shard_map/ppermute | solution.py:70
  141.2 10.6 %collective-permute-start.18 = (bf16[64,2048]{1,0:T(8,128)(2,1)S(1)}, bf16[64,2048]{1,0:T(8,128)(2,1)S(1)}, u32[]{:S(2)}, u32[]{:S(2)}) collective-permute-start(bf16[64,2048]{1,0:T(8,128)(2,1)S(1)} %get-tuple-element.115), channel_id=1, source_target_pairs={{0,1},{1,2},{2,3},{3,0},{4,5},{5,6},{6,7},{7,4},{8,9},{9,10},{10,1... | collective-permute-start | bytes 786440 | tf_op jit(solution)/shard_map/ppermute | solution.py:70
  158.7 7.4 %collective-permute-start.21 = (bf16[64,2048]{1,0:T(8,128)(2,1)S(1)}, bf16[64,2048]{1,0:T(8,128)(2,1)S(1)}, u32[]{:S(2)}, u32[]{:S(2)}) collective-permute-start(bf16[64,2048]{1,0:T(8,128)(2,1)S(1)} %get-tuple-element.131), channel_id=1, source_target_pairs={{0,1},{1,2},{2,3},{3,0},{4,5},{5,6},{6,7},{7,4},{8,9},{9,10},{10,1... | collective-permute-start | bytes 786440 | tf_op jit(solution)/shard_map/ppermute | solution.py:70
  159.4 8.5 %collective-permute-start.22 = (bf16[64,2048]{1,0:T(8,128)(2,1)S(1)}, bf16[64,2048]{1,0:T(8,128)(2,1)S(1)}, u32[]{:S(2)}, u32[]{:S(2)}) collective-permute-start(bf16[64,2048]{1,0:T(8,128)(2,1)S(1)} %get-tuple-element.130), channel_id=1, source_target_pairs={{0,1},{1,2},{2,3},{3,0},{4,5},{5,6},{6,7},{7,4},{8,9},{9,10},{10,1... | collective-permute-start | bytes 786440 | tf_op jit(solution)/shard_map/ppermute | solution.py:70
  160.7 7.9 %collective-permute-start.23 = (bf16[64,2048]{1,0:T(8,128)(2,1)S(1)}, bf16[64,2048]{1,0:T(8,128)(2,1)S(1)}, u32[]{:S(2)}, u32[]{:S(2)}) collective-permute-start(bf16[64,2048]{1,0:T(8,128)(2,1)S(1)} %get-tuple-element.131), channel_id=1, source_target_pairs={{0,3},{1,0},{2,1},{3,2},{4,7},{5,4},{6,5},{7,6},{8,11},{9,8},{10,9... | collective-permute-start | bytes 786440 | tf_op jit(solution)/shard_map/ppermute | solution.py:70
  163.8 10.7 %collective-permute-start.26 = (bf16[64,2048]{1,0:T(8,128)(2,1)S(1)}, bf16[64,2048]{1,0:T(8,128)(2,1)S(1)}, u32[]{:S(2)}, u32[]{:S(2)}) collective-permute-start(bf16[64,2048]{1,0:T(8,128)(2,1)S(1)} %collective-permute-done.24), channel_id=1, source_target_pairs={{0,3},{1,0},{2,1},{3,2},{4,7},{5,4},{6,5},{7,6},{8,11},{9,8},{10,9... | collective-permute-start | bytes 786440 | tf_op jit(solution)/shard_map/ppermute | solution.py:70
  166.1 7.7 %collective-permute-start.25 = (bf16[64,2048]{1,0:T(8,128)(2,1)S(1)}, bf16[64,2048]{1,0:T(8,128)(2,1)S(1)}, u32[]{:S(2)}, u32[]{:S(2)}) collective-permute-start(bf16[64,2048]{1,0:T(8,128)(2,1)S(1)} %collective-permute-done.21), channel_id=1, source_target_pairs={{0,1},{1,2},{2,3},{3,0},{4,5},{5,6},{6,7},{7,4},{8,9},{9,10},{10,1... | collective-permute-start | bytes 786440 | tf_op jit(solution)/shard_map/ppermute | solution.py:70
  196.8 26.1 %all-to-all-start.2 = ((bf16[4,128,2048]{2,1,0:T(8,128)(2,1)}), bf16[4,128,2048]{2,1,0:T(8,128)(2,1)}, u32[]{:S(2)}, u32[]{:S(2)}) async-start(bf16[4,128,2048]{2,1,0:T(8,128)(2,1)} %bitcast.118), calls=%async_computation.2 | async-start | bytes 4194304 | tf_op jit(solution)/shard_map/all_to_all | solution.py:66
  201.2 121.9 %reduce-scatter.3.cloned.1.call-start = ((), (), s32[]{:S(2)}) async-start(), calls=%async_computation.13 | async-start | bytes 18874368 | tf_op jit(solution)/shard_map/reduce_scatter | solution.py:120
  238.7 6.8 %collective-permute-start.27 = (bf16[64,2048]{1,0:T(8,128)(2,1)S(1)}, bf16[64,2048]{1,0:T(8,128)(2,1)S(1)}, u32[]{:S(2)}, u32[]{:S(2)}) collective-permute-start(bf16[64,2048]{1,0:T(8,128)(2,1)S(1)} %get-tuple-element.129), channel_id=1, source_target_pairs={{0,1},{1,2},{2,3},{3,0},{4,5},{5,6},{6,7},{7,4},{8,9},{9,10},{10,1... | collective-permute-start | bytes 786440 | tf_op jit(solution)/shard_map/ppermute | solution.py:70
  238.9 9.4 %collective-permute-start.28 = (bf16[64,2048]{1,0:T(8,128)(2,1)S(1)}, bf16[64,2048]{1,0:T(8,128)(2,1)S(1)}, u32[]{:S(2)}, u32[]{:S(2)}) collective-permute-start(bf16[64,2048]{1,0:T(8,128)(2,1)S(1)} %get-tuple-element.128), channel_id=1, source_target_pairs={{0,1},{1,2},{2,3},{3,0},{4,5},{5,6},{6,7},{7,4},{8,9},{9,10},{10,1... | collective-permute-start | bytes 786440 | tf_op jit(solution)/shard_map/ppermute | solution.py:70
  239.2 9.8 %collective-permute-start.29 = (bf16[64,2048]{1,0:T(8,128)(2,1)S(1)}, bf16[64,2048]{1,0:T(8,128)(2,1)S(1)}, u32[]{:S(2)}, u32[]{:S(2)}) collective-permute-start(bf16[64,2048]{1,0:T(8,128)(2,1)S(1)} %get-tuple-element.129), channel_id=1, source_target_pairs={{0,3},{1,0},{2,1},{3,2},{4,7},{5,4},{6,5},{7,6},{8,11},{9,8},{10,9... | collective-permute-start | bytes 786440 | tf_op jit(solution)/shard_map/ppermute | solution.py:70
  242.6 10.5 %collective-permute-start.32 = (bf16[64,2048]{1,0:T(8,128)(2,1)S(1)}, bf16[64,2048]{1,0:T(8,128)(2,1)S(1)}, u32[]{:S(2)}, u32[]{:S(2)}) collective-permute-start(bf16[64,2048]{1,0:T(8,128)(2,1)S(1)} %collective-permute-done.30), channel_id=1, source_target_pairs={{0,3},{1,0},{2,1},{3,2},{4,7},{5,4},{6,5},{7,6},{8,11},{9,8},{10,9... | collective-permute-start | bytes 786440 | tf_op jit(solution)/shard_map/ppermute | solution.py:70
  245.5 6.8 %collective-permute-start.31 = (bf16[64,2048]{1,0:T(8,128)(2,1)S(1)}, bf16[64,2048]{1,0:T(8,128)(2,1)S(1)}, u32[]{:S(2)}, u32[]{:S(2)}) collective-permute-start(bf16[64,2048]{1,0:T(8,128)(2,1)S(1)} %collective-permute-done.27), channel_id=1, source_target_pairs={{0,1},{1,2},{2,3},{3,0},{4,5},{5,6},{6,7},{7,4},{8,9},{9,10},{10,1... | collective-permute-start | bytes 786440 | tf_op jit(solution)/shard_map/ppermute | solution.py:70
  259.6 10.8 %all-to-all-start.3 = ((bf16[4,512,128]{2,1,0:T(8,128)(2,1)}), bf16[4,512,128]{2,1,0:T(8,128)(2,1)S(1)}, u32[]{:S(2)}, u32[]{:S(2)}) async-start(bf16[4,512,128]{2,1,0:T(8,128)(2,1)} %shard_map.338), calls=%async_computation.3 | async-start | bytes 1048576 | tf_op jit(solution)/shard_map/all_to_all | solution.py:66
  283.4 24.8 %all-to-all-start.4 = ((bf16[4,512,384]{2,1,0:T(8,128)(2,1)}), bf16[4,512,384]{2,1,0:T(8,128)(2,1)}, u32[]{:S(2)}, u32[]{:S(2)}) async-start(bf16[4,512,384]{2,1,0:T(8,128)(2,1)} %bitcast.25), calls=%async_computation.4 | async-start | bytes 3145728 | tf_op jit(solution)/shard_map/all_to_all | solution.py:66
  290.2 10.0 %collective-permute-start.33 = (bf16[128,2048]{1,0:T(8,128)(2,1)}, bf16[128,2048]{1,0:T(8,128)(2,1)S(1)}, u32[]{:S(2)}, u32[]{:S(2)}) collective-permute-start(bf16[128,2048]{1,0:T(8,128)(2,1)} %get-tuple-element.108), channel_id=1, source_target_pairs={{0,3},{1,0},{2,1},{3,2},{4,7},{5,4},{6,5},{7,6},{8,11},{9,8},{10,9... | collective-permute-start | bytes 1572872 | tf_op jit(solution)/shard_map/ppermute | solution.py:70
  290.2 10.0 %collective-permute-start.35 = (bf16[128,2048]{1,0:T(8,128)(2,1)S(1)}, bf16[128,2048]{1,0:T(8,128)(2,1)S(1)}, u32[]{:S(2)}, u32[]{:S(2)}) collective-permute-start(bf16[128,2048]{1,0:T(8,128)(2,1)S(1)} %get-tuple-element.109), channel_id=1, source_target_pairs={{0,2},{1,3},{2,0},{3,1},{4,6},{5,7},{6,4},{7,5},{8,10},{9,11},{10,... | collective-permute-start | bytes 1572872 | tf_op jit(solution)/shard_map/ppermute | solution.py:70
  290.7 15.1 %collective-permute-start.34 = (bf16[128,2048]{1,0:T(8,128)(2,1)S(1)}, bf16[128,2048]{1,0:T(8,128)(2,1)}, u32[]{:S(2)}, u32[]{:S(2)}) collective-permute-start(bf16[128,2048]{1,0:T(8,128)(2,1)S(1)} %get-tuple-element.110), channel_id=1, source_target_pairs={{0,1},{1,2},{2,3},{3,0},{4,5},{5,6},{6,7},{7,4},{8,9},{9,10},{10,1... | collective-permute-start | bytes 1572872 | tf_op jit(solution)/shard_map/ppermute | solution.py:70
  308.2 13.0 %all-to-all-start.5 = ((f32[16,8,128]{2,1,0:T(8,128)}), f32[16,8,128]{2,1,0:T(8,128)S(1)}, u32[]{:S(2)}, u32[]{:S(2)}) async-start(f32[16,8,128]{2,1,0:T(8,128)} %bitcast.34), calls=%async_computation.5 | async-start | bytes 131072 | tf_op jit(solution)/shard_map/all_to_all | solution.py:62
  312.9 79.8 %reduce-scatter.5.cloned.1.call-start = ((), (), s32[]{:S(2)}) async-start(), calls=%async_computation.14 | async-start | bytes 9437184 | tf_op jit(solution)/shard_map/reduce_scatter | solution.py:120
  323.8 29.7 %all-to-all-start.6 = ((f32[8,8,128]{2,1,0:T(8,128)}), f32[8,8,128]{2,1,0:T(8,128)S(1)}, u32[]{:S(2)}, u32[]{:S(2)}) async-start(f32[8,8,128]{2,1,0:T(8,128)} %broadcast_in_dim.20), calls=%async_computation.7 | async-start | bytes 65536 | tf_op jit(solution)/shard_map/all_to_all | solution.py:58
  353.6 39.1 %all-to-all-start.7 = ((bf16[4,128,2048]{2,1,0:T(8,128)(2,1)}), bf16[4,128,2048]{2,1,0:T(8,128)(2,1)S(1)}, u32[]{:S(2)}, u32[]{:S(2)}) async-start(bf16[4,128,2048]{2,1,0:T(8,128)(2,1)} %bitcast.115), calls=%async_computation.8 | async-start | bytes 4194304 | tf_op jit(solution)/shard_map/all_to_all | solution.py:66
  360.6 25.0 %collective-permute-start.39 = (bf16[256,1024]{1,0:T(8,128)(2,1)}, bf16[256,1024]{1,0:T(8,128)(2,1)S(1)}, u32[]{:S(2)}, u32[]{:S(2)}) collective-permute-start(bf16[256,1024]{1,0:T(8,128)(2,1)} %get-tuple-element.105), channel_id=1, source_target_pairs={{0,12},{4,0},{8,4},{12,8},{1,13},{5,1},{9,5},{13,9},{2,14},{6,2},{... | collective-permute-start | bytes 1572872 | tf_op jit(solution)/shard_map/ppermute | solution.py:70
  363.0 22.6 %collective-permute-start.41 = (bf16[256,1024]{1,0:T(8,128)(2,1)}, bf16[256,1024]{1,0:T(8,128)(2,1)}, u32[]{:S(2)}, u32[]{:S(2)}) collective-permute-start(bf16[256,1024]{1,0:T(8,128)(2,1)} %get-tuple-element.106), channel_id=1, source_target_pairs={{0,8},{4,12},{8,0},{12,4},{1,9},{5,13},{9,1},{13,5},{2,10},{6,14},... | collective-permute-start | bytes 1572872 | tf_op jit(solution)/shard_map/ppermute | solution.py:70
  363.6 26.3 %collective-permute-start.40 = (bf16[256,1024]{1,0:T(8,128)(2,1)}, bf16[256,1024]{1,0:T(8,128)(2,1)}, u32[]{:S(2)}, u32[]{:S(2)}) collective-permute-start(bf16[256,1024]{1,0:T(8,128)(2,1)} %get-tuple-element.107), channel_id=1, source_target_pairs={{0,4},{4,8},{8,12},{12,0},{1,5},{5,9},{9,13},{13,1},{2,6},{6,10},{... | collective-permute-start | bytes 1572872 | tf_op jit(solution)/shard_map/ppermute | solution.py:70
  393.9 12.7 %collective-permute-start.36 = (bf16[256,512]{1,0:T(8,128)(2,1)S(1)}, bf16[256,512]{1,0:T(8,128)(2,1)}, u32[]{:S(2)}, u32[]{:S(2)}) collective-permute-start(bf16[256,512]{1,0:T(8,128)(2,1)S(1)} %get-tuple-element.119), channel_id=1, source_target_pairs={{0,12},{4,0},{8,4},{12,8},{1,13},{5,1},{9,5},{13,9},{2,14},{6,2},{... | collective-permute-start | bytes 786440 | tf_op jit(solution)/shard_map/ppermute | solution.py:70
  396.1 10.6 %collective-permute-start.38 = (bf16[256,512]{1,0:T(8,128)(2,1)S(1)}, bf16[256,512]{1,0:T(8,128)(2,1)}, u32[]{:S(2)}, u32[]{:S(2)}) collective-permute-start(bf16[256,512]{1,0:T(8,128)(2,1)S(1)} %get-tuple-element.120), channel_id=1, source_target_pairs={{0,8},{4,12},{8,0},{12,4},{1,9},{5,13},{9,1},{13,5},{2,10},{6,14},... | collective-permute-start | bytes 786440 | tf_op jit(solution)/shard_map/ppermute | solution.py:70
  396.6 14.9 %collective-permute-start.37 = (bf16[256,512]{1,0:T(8,128)(2,1)S(1)}, bf16[256,512]{1,0:T(8,128)(2,1)}, u32[]{:S(2)}, u32[]{:S(2)}) collective-permute-start(bf16[256,512]{1,0:T(8,128)(2,1)S(1)} %get-tuple-element.121), channel_id=1, source_target_pairs={{0,4},{4,8},{8,12},{12,0},{1,5},{5,9},{9,13},{13,1},{2,6},{6,10},{... | collective-permute-start | bytes 786440 | tf_op jit(solution)/shard_map/ppermute | solution.py:70
  400.7 15.1 %all-to-all-start.8 = ((f32[16,42,128]{2,1,0:T(8,128)}), f32[16,42,128]{2,1,0:T(8,128)S(1)}, u32[]{:S(2)}, u32[]{:S(2)}) async-start(f32[16,42,128]{2,1,0:T(8,128)} %broadcast_in_dim.22), calls=%async_computation.10 | async-start | bytes 786432 | tf_op jit(solution)/shard_map/all_to_all | solution.py:58
  416.6 13.1 %all-to-all-start.9 = ((f32[8,64,128]{2,1,0:T(8,128)}), f32[8,64,128]{2,1,0:T(8,128)S(1)}, u32[]{:S(2)}, u32[]{:S(2)}) async-start(f32[8,64,128]{2,1,0:T(8,128)} %broadcast_in_dim.23), calls=%async_computation.11 | async-start | bytes 524288 | tf_op jit(solution)/shard_map/all_to_all | solution.py:58
  (32 other events, 214.3 us)
Sparse Core Ops, SparseCore 0:
  10.9 59.7 all-gather.3
  72.4 84.7 all-gather.5
  223.0 100.1 reduce-scatter.2
  325.4 66.8 reduce-scatter.4
where the time goes:
time: 445 us; the launch traced here: 438 us
  waiting for transfers between devices  135 us (30%)
  Pallas kernels  110 us (25%)
  starting transfers between devices  103 us (23%)
  local copies, waits for them, and re-layouts  40.1 us (9%)
  between operations  23.2 us (5%)
  other arithmetic  15.4 us (3%)
  blocking collectives  10 us (2%)
    ppermute x42, waiting for transfers between devices, ring(): lax.ppermute(array, axis, [(i, (i + step) % RING) for i in range(RING)])  93.7 us
    ppermute x42, starting transfers between devices, ring(): lax.ppermute(array, axis, [(i, (i + step) % RING) for i in range(RING)])  44 us
    all_to_all x3, starting transfers between devices, spread(): lax.all_to_all(jnp.broadcast_to(array[None], (size,) + array.shape), axes...  33 us
    all_to_all x5, starting transfers between devices, swap(): return lax.all_to_all(parts, axes, 0, 0)  21.6 us
    pallas_call x1, Pallas kernels, ffn_second(): call(ffn_second_body, (struct((count, width), LOW), struct(weight.shape,...  21.5 us
    pallas_call x1, Pallas kernels, ffn_first(): call(ffn_first_body, (struct((count, xs * size), LOW), struct((count, xs...  21.5 us
    all_gather x1, waiting for transfers between devices, gather_weight(): full = lax.all_gather(shard, ('z', 'c', 'x'), axis=0)  19.5 us
    unnamed x78, local copies, waits for them, and re-layouts  18.6 us
  transfers between devices with their start and end apart: 55, of which 28 were waited for; matrix products, arithmetic and copies ran while one was open for 10% of the time, Pallas kernels for 20%

commit v1 on v0

--- a/solution.py
+++ b/solution.py
@@ -67,11 +67,9 @@
 
 
 def ring(array, step, axis="y"):
+    if step == 0:
+        return array
     return lax.ppermute(array, axis, [(i, (i + step) % RING) for i in range(RING)])
-
-
-def ring_stack(array, axis):
-    return jnp.stack([array] + [ring(array, step, axis) for step in (1, -1, 2)])
 
 
 def ring_collect(parts, axis):
@@ -79,22 +77,25 @@
     return sum(term.astype(WIDE) for term in [parts[0]] + came)
 
 
-def ring_gather(rows):
+def ring_gather(rows, beside=None):
     half = rows.shape[0] // 2
     first, second = rows[:half], rows[half:]
     before_first, after_second = ring(first, 1), ring(second, -1)
     before_second, after_first = ring(second, 1), ring(first, -1)
+    if beside is not None:
+        before_first, after_second, beside = tie(before_first, after_second, beside)
     across_first, across_second = ring(before_first, 1), ring(after_second, -1)
-    return jnp.concatenate(
+    gathered = jnp.concatenate(
         [
             first, second, before_first, before_second,
             after_first, after_second, across_first, across_second,
         ],
         0,
     )
-
-
-def ring_sum(rows):
+    return gathered if beside is None else (gathered, beside)
+
+
+def ring_sum_parts(rows):
     own = rows.shape[0] // RING
     half = own // 2
     start, before, after, across = (rows[i * own : (i + 1) * own] for i in range(RING))
@@ -102,6 +103,12 @@
     second_after, first_before = ring(after[half:], 1), ring(before[:half], -1)
     first_after = ring((after[:half].astype(WIDE) + from_before.astype(WIDE)).astype(LOW), 1)
     second_before = ring((before[half:].astype(WIDE) + from_after.astype(WIDE)).astype(LOW), -1)
+    return (start, first_after, second_after, first_before, second_before)
+
+
+def ring_sum(rows):
+    start, first_after, second_after, first_before, second_before = ring_sum_parts(rows)
+    half = first_after.shape[0]
     first = start[:half].astype(WIDE) + first_after.astype(WIDE) + first_before.astype(WIDE)
     second = start[half:].astype(WIDE) + second_after.astype(WIDE) + second_before.astype(WIDE)
     return jnp.concatenate([first, second], 0)
@@ -291,7 +298,7 @@
 
 
 def ffn_second_body(
-    norm_ref, cot_ref, hidden_ref, grad_up_ref, down_ref, branch_ref, weight_grad_ref, total
+    place_ref, norm_ref, cot_ref, hidden_ref, grad_up_ref, down_ref, branch_ref, weight_grad_ref, total
 ):
     width, cols = norm_ref.shape[1], down_ref.shape[-1]
     zc, piece, _ = weight_grad_ref.shape
@@ -307,23 +314,24 @@
         branch_ref[...] = total[...].astype(LOW)
 
 
-def ffn_second(norm_rows, cot_rows, hidden, grad_up, weight):
+def ffn_second(places, norm_rows, cot_rows, hidden, grad_up, weight):
     count, width = norm_rows.shape
     zc, xs, piece, cols = weight.shape
     size = cols // 2
     rows = whole((count, width))
-    wide = pl.BlockSpec((count, size), lambda i: (0, i))
+    wide = pl.BlockSpec((count, size), lambda i, *_: (0, i))
     return call(
         ffn_second_body,
         (struct((count, width), LOW), struct(weight.shape, LOW)),
         (xs,),
-        [rows, rows, wide, wide, pl.BlockSpec((zc, None, piece, size), lambda i: (0, i, 0, 1))],
-        (rows, pl.BlockSpec((zc, None, piece, cols), lambda i: (0, i, 0, 0))),
+        [rows, rows, wide, wide, pl.BlockSpec((zc, None, piece, size), lambda i, *_: (0, i, 0, 1))],
+        (rows, pl.BlockSpec((zc, None, piece, cols), lambda i, places: (0, places[i], 0, 0))),
         6 * count * width * xs * size,
         40 * 2**20,
         scratch=[pltpu.VMEM((count, width), WIDE)],
+        prefetch=1,
         vmem=56,
-    )(norm_rows, cot_rows, hidden, grad_up, weight)
+    )(places, norm_rows, cot_rows, hidden, grad_up, weight)
 
 
 def only_head(array, head):
@@ -506,10 +514,20 @@
     return (centered * inverse * gain_vec + shift_vec).astype(LOW)
 
 
-def norm_back_body(with_low, parts_ref, rows_ref, grad_ref, gain_ref, *refs):
-    gradient = parts_ref[0].astype(WIDE)
-    for part in range(1, parts_ref.shape[0]):
-        gradient += parts_ref[part].astype(WIDE)
+def norm_back_body(count, with_low, *refs):
+    parts, (rows_ref, grad_ref, gain_ref) = refs[:count], refs[count : count + 3]
+    refs = refs[count + 3 :]
+    if count == 1:
+        terms = [parts[0][i] for i in range(parts[0].shape[0])]
+    else:
+        start, first_after, second_after, first_before, second_before = (p[...] for p in parts)
+        early = pl.program_id(0) < pl.num_programs(0) // 2
+        terms = [
+            start,
+            jnp.where(early, first_after, second_after),
+            jnp.where(early, first_before, second_before),
+        ]
+    gradient = sum(term.astype(WIDE) for term in terms)
     values = rows_ref[...].astype(WIDE)
     centered = values - jnp.mean(values, 1, keepdims=True)
     inverse = lax.rsqrt(jnp.mean(centered * centered, 1, keepdims=True) + 1e-05)
@@ -534,15 +552,20 @@
 
 
 def norm_back(parts, rows, grad, gain, keep=None):
-    count, own, width = parts.shape
+    own, width = rows.shape
     step = own // 4
     flat = pl.BlockSpec((step, width), lambda i: (i, 0))
     sums = pl.BlockSpec((8, width), lambda i: (0, 0))
-    in_specs = [
-        pl.BlockSpec((count, step, width), lambda i: (0, i, 0)), flat, flat,
-        pl.BlockSpec((1, width), lambda i: (0, 0)),
-    ]
-    args = [parts, rows, grad, gain.reshape(1, width)]
+    if isinstance(parts, tuple):
+        early = pl.BlockSpec((step, width), lambda i: (jnp.minimum(i, 1), 0))
+        late = pl.BlockSpec((step, width), lambda i: (jnp.maximum(i - 2, 0), 0))
+        in_specs, args = [flat, early, late, early, late], list(parts)
+    else:
+        in_specs = [pl.BlockSpec((parts.shape[0], step, width), lambda i: (0, i, 0))]
+        args = [parts]
+    count = len(args)
+    in_specs += [flat, flat, pl.BlockSpec((1, width), lambda i: (0, 0))]
+    args += [rows, grad, gain.reshape(1, width)]
     outs, specs = [struct((own, width), WIDE)], [flat]
     if keep is not None:
         in_specs.append(pl.BlockSpec((step, 1), lambda i: (i, 0)))
@@ -550,7 +573,7 @@
         outs.append(struct((own, width), LOW))
         specs.append(flat)
     return call(
-        partial(norm_back_body, keep is not None),
+        partial(norm_back_body, count, keep is not None),
         tuple(outs + [struct((8, width), WIDE)]),
         (own // step,),
         in_specs,
@@ -560,25 +583,18 @@
     )(*args)
 
 
-def split_back(flat, vectors):
+def collect_vectors(vectors):
+    flat = jnp.concatenate([v.reshape(-1) for v in vectors])
+    return collect(flat.reshape(16, -1, 128), COLS)
+
+
+def spread_vectors(part, sizes):
+    flat = spread(jnp.sum(spread(part, ROWS, 8), 0), COLS, 16).reshape(-1)
     pieces, start = [], 0
-    for v in vectors:
-        pieces.append(flat[start : start + v.size])
-        start += v.size
+    for size in sizes:
+        pieces.append(flat[start : start + size])
+        start += size
     return pieces
-
-
-def last_totals(vectors, columns, ready):
-    shared = jnp.concatenate([v.reshape(-1, 128) for v in vectors], 0)
-    rows, more = shared.shape[0], columns.shape[0]
-    parts = spread(jnp.concatenate([shared, columns, ready], 0), COLS, 16)
-    part = jnp.sum(parts[:, :rows], 0)
-    part = jnp.concatenate([part, parts[:, rows : rows + more].reshape(-1, 128)], 0)
-    part = jnp.sum(spread(part, ROWS, 8), 0)
-    placed = part[rows:].reshape(16, more, 128)
-    totals = split_back(part[:rows].reshape(-1), vectors)
-    totals += [placed[:, i].reshape(-1) for i in range(more)]
-    return totals, parts[:, rows + more :]
 
 
 def shards(
@@ -615,8 +631,10 @@
     norm1 = ring_gather(norm_rows(inputs, ln1_gain, ln1_shift))
     flat_cot = cotangent.reshape(own, width)
     g_ffn = (keep * flat_cot.astype(WIDE)).astype(LOW)
-    norm1, w_ff = tie(norm1, ring_stack(w_ff, "x"))
-    w_ff = lax.all_gather(w_ff, ROWS, axis=0)
+    norm1, g_ffn, w_ff = tie(norm1, g_ffn, w_ff)
+    cot_rows, w_ff = ring_gather(g_ffn, [ring(w_ff, step, "x") for step in (0, 1, -1, 2)])
+    w_ff = lax.all_gather(jnp.stack(w_ff), ROWS, axis=0)
+    norm1, cot_rows = tie(norm1, cot_rows)
 
     def mine(vector, cols):
         return lax.dynamic_index_in_dim(vector.reshape(RING, RING, cols), y_at, 1, False)
@@ -626,11 +644,8 @@
     ).reshape(RING, 1, 3 * head_cols)
     qkv = qkv_project(norm1, w_attn, bias)
     rows5 = (RING, RING, seqs, own_rows)
-    qkv, g_ffn = tie(qkv, g_ffn)
-    cot_rows = ring_gather(g_ffn)
     qkv = swap(qkv, "x").reshape(rows5 + (3 * head_cols,))
     heads, exact, logs = attend(live_counts, qkv, head_cols)
-    heads, cot_rows = tie(heads, cot_rows)
     heads = swap(heads.reshape(RING, RING * own, head_cols), "x")
     branch1 = ring_sum(out_project(slots, heads, w_attn, 3, 4)) + out_bias
     middle = inputs + keep * branch1
@@ -640,7 +655,7 @@
     hidden, grad_up, g_norm2, up_bias_part = ffn_first(places, norm2, cot_rows, w_ff, ff_bias)
     g_norm2 = swap(g_norm2.reshape(RING, own, width), "y")
     g_norm2, branch2, ff_grad = tie(
-        g_norm2, *ffn_second(norm2, cot_rows, hidden, grad_up, w_ff)
+        g_norm2, *ffn_second(x_places, norm2, cot_rows, hidden, grad_up, w_ff)
     )
     ff_grad = settle(ff_grad)
     grad_mid, g_attn, sums2 = norm_back(g_norm2, middle, flat_cot, ln2_gain, keep)
@@ -666,28 +681,29 @@
         up_bias_full,
         jnp.sum(g_ffn.astype(WIDE), 0),
     )
-    early_flat = jnp.concatenate([v.reshape(-1) for v in early]).reshape(16, -1, 128)
-    d_qkv, attn_grad, result, early_flat = tie(d_qkv, attn_grad, result, early_flat)
-    part = collect(early_flat, COLS)
+    d_qkv, attn_grad, result = tie(d_qkv, attn_grad, result)
     attn_grad = weight_grads(norm1, d_qkv, 4 * head_cols, 0, attn_grad)
-    d_qkv, attn_grad, part, ff_grad = tie(d_qkv, attn_grad, part, ff_grad)
+    d_qkv, attn_grad, ff_grad = tie(d_qkv, attn_grad, ff_grad)
     attn_grad = settle(attn_grad)
-    part = jnp.sum(spread(part, ROWS, 8), 0)
-    g_norm1 = out_project(places, d_qkv, w_attn, 0, 2)
-    g_norm1, part = tie(g_norm1, part)
-    ff_grad = ring_collect(ff_grad, "x")
-    g_norm1 = swap(g_norm1.reshape(RING, own, width), "y")
-    g_norm1, attn_grad = tie(g_norm1, attn_grad)
-    here = [lax.dynamic_index_in_dim(attn_grad, x_places[i], 0, False) for i in range(RING)]
-    attn_grad = ring_collect(here, "x")
+    g_norm1 = ring_sum_parts(out_project(slots, d_qkv, w_attn, 0, 2))
+    g_norm1, ff_grad = tie(g_norm1, swap(ff_grad, "x"))
+    ff_grad = jnp.sum(ff_grad.astype(WIDE), 0)
     grad_tokens, sums1 = norm_back(g_norm1, tokens.reshape(own, width), grad_mid, ln1_gain)
     grad_tokens = grad_tokens.reshape(tokens.shape)
     d_sums = jnp.sum(d_sums, 0).reshape(3, head_cols)
-    ln1_totals, early_totals = last_totals((sums1[0], sums1[1]), d_sums[::2], part)
-    ln1_gain_sum, ln1_shift_sum, q_bias_sum, v_bias_sum = ln1_totals
-    out_bias_sum, ln2_gain_sum, ln2_shift_sum, up_bias_sum, down_bias_sum = split_back(
-        early_totals.reshape(-1), early
-    )
+
+    def placed(row):
+        blank = jnp.zeros((RING * RING, head_cols), WIDE)
+        return lax.dynamic_update_slice_in_dim(blank, row[None], head_at, 0)
+
+    part = collect_vectors(early + (sums1[0], sums1[1], placed(d_sums[0]), placed(d_sums[2])))
+    part, attn_grad = tie(part, attn_grad)
+    here = [lax.dynamic_index_in_dim(attn_grad, x_places[i], 0, False) for i in range(RING)]
+    attn_grad = ring_collect(here, "x")
+    sizes = (width, width, width, RING * RING * ff_cols) + (width,) * 5
+    totals = spread_vectors(part, sizes)
+    out_bias_sum, ln2_gain_sum, ln2_shift_sum, up_bias_sum, down_bias_sum = totals[:5]
+    ln1_gain_sum, ln1_shift_sum, q_bias_sum, v_bias_sum = totals[5:]
     return (
         result,
         grad_tokens,

time: 445 us -> 451 us (1.013)
  starting transfers between devices: 103 us -> 89.6 us
  blocking collectives: 10 us -> 20.6 us
    all_to_all x3 -> x2, starting transfers between devices: 33 us -> 12.8 us  [spread(): lax.all_to_all(jnp.broadcast_to(array[None], (size,) + array.shape), axes...]
    all_gather x1, waiting for transfers between devices: 19.5 us -> 0.01 us  [gather_weight(): full = lax.all_gather(shard, ('z', 'c', 'x'), axis=0)]
    reduce_scatter x2, waiting for transfers between devices: 1.95 us -> 20.7 us  [settle(): return lax.psum_scatter(gradient, ROWS, scatter_dimension=0)]
    all_to_all x1 -> x2, blocking collectives: 10 us -> 20.6 us  [swap(): return lax.all_to_all(parts, axes, 0, 0)]
    ppermute x42 -> x45, starting transfers between devices: 44 us -> 51.7 us  [ring(): lax.ppermute(array, axis, [(i, (i + step) % RING) for i in range(RING)])]
    ppermute x42 -> x45, waiting for transfers between devices: 93.7 us -> 87.1 us  [ring(): lax.ppermute(array, axis, [(i, (i + step) % RING) for i in range(RING)])]
    all_to_all x1, waiting for transfers between devices: 0.01 us -> 4.54 us  [collect(): return jnp.sum(lax.all_to_all(parts, axes, 0, 0).astype(WIDE), 0)]
    all_to_all x3 -> x2, waiting for transfers between devices: 7.42 us -> 10.6 us  [spread(): lax.all_to_all(jnp.broadcast_to(array[None], (size,) + array.shape), axes...]
  transfers between devices with their start and end apart: 55 -> 56, of which waited for: 28 -> 30; matrix products, arithmetic and copies ran while one was open for 10% -> 12% of each run, Pallas kernels for 20% -> 21%
where the time goes in v1:
time: 451 us; the launch traced here: 444 us
  waiting for transfers between devices  138 us (31%)
  Pallas kernels  113 us (25%)
  starting transfers between devices  89.6 us (20%)
  local copies, waits for them, and re-layouts  41.2 us (9%)
  between operations  23.2 us (5%)
  blocking collectives  20.6 us (5%)
  other arithmetic  19.1 us (4%)
    ppermute x45, waiting for transfers between devices, ring(): lax.ppermute(array, axis, [(i, (i + step) % RING) for i in range(RING)])  87.1 us
    ppermute x45, starting transfers between devices, ring(): lax.ppermute(array, axis, [(i, (i + step) % RING) for i in range(RING)])  51.7 us
    pallas_call x1, Pallas kernels, ffn_second(): call(ffn_second_body, (struct((count, width), LOW), struct(weight.shape,...  22.2 us
    pallas_call x1, Pallas kernels, ffn_first(): call(ffn_first_body, (struct((count, xs * size), LOW), struct((count, xs...  21.4 us
    reduce_scatter x2, waiting for transfers between devices, settle(): return lax.psum_scatter(gradient, ROWS, scatter_dimension=0)  20.7 us
    all_to_all x4, starting transfers between devices, swap(): return lax.all_to_all(parts, axes, 0, 0)  20.6 us
    all_to_all x2, blocking collectives, swap(): return lax.all_to_all(parts, axes, 0, 0)  20.6 us
    unnamed x92, local copies, waits for them, and re-layouts  18.8 us
  transfers between devices with their start and end apart: 56, of which 30 were waited for; matrix products, arithmetic and copies ran while one was open for 12% of the time, Pallas kernels for 21%

profile of v1, /device:TPU:1, one launch (start us, length us, event | category | flops | bytes accessed | tf_op | source)
XLA Modules:
  0.0 443.9 jit_solution(1655344145468609917)
XLA Ops:
  13.0 3.6 collective-permute-start.3
  16.6 2.7 collective-permute-start.2
  21.8 3.3 collective-permute-start.5
  25.2 5.4 %collective-permute-done = bf16[64,2048]{1,0:T(8,128)(2,1)} collective-permute-done((bf16[64,2048]{1,0:T(8,128)(2,1)}, bf16[64,2048]{1,0:T(8,128)(2,1)}, u32[]{:S(2)}, u32[]{:S(2)}) %collective-permute-start) | collective-permute-done | bytes 262176 | tf_op jit(solution)/shard_map/ppermute | solution.py:72
  33.6 4.4 collective-permute-done.4
  38.0 2.8 collective-permute-start.10
  43.9 4.2 collective-permute-done.7
  49.3 4.2 collective-permute-done.10
  53.5 21.5 %collective-permute-done.9 = bf16[256,1024]{1,0:T(8,128)(2,1)S(1)} collective-permute-done((bf16[256,1024]{1,0:T(8,128)(2,1)S(1)}, bf16[256,1024]{1,0:T(8,128)(2,1)S(1)}, u32[]{:S(2)}, u32[]{:S(2)}) %collective-permute-start.9) | collective-permute-done | bytes 524320 | tf_op jit(solution)/shard_map/ppermute | solution.py:72
  78.9 2.7 collective-permute-start.12
  82.4 2.7 collective-permute-start.14
  90.3 8.6 %shard_map.332 = bf16[4,512,384]{2,1,0:T(8,128)(2,1)} custom-call(bf16[512,2048]{1,0:T(8,128)(2,1)} %copy-done.8, bf16[8,4,256,512]{3,2,1,0:T(8,128)(2,1)} %bitcast.80, f32[4,1,384]{2,1,0:T(1,128)} %reshape.293.bias_ref), custom_call_target="tpu_custom_call" | custom-call | flops 3221225472 | bytes 10485760 | tf_op jit(solution)/shard_map/pallas_call | solution.py:139
  98.9 7.2 %all-to-all-start = ((bf16[4,512,384]{2,1,0:T(8,128)(2,1)}), bf16[4,512,384]{2,1,0:T(8,128)(2,1)}, u32[]{:S(2)}, u32[]{:S(2)}) async-start(bf16[4,512,384]{2,1,0:T(8,128)(2,1)} %shard_map.332), calls=%async_computation | async-start | bytes 3145728 | tf_op jit(solution)/shard_map/all_to_all | solution.py:66
  106.2 14.7 %all-to-all-done = bf16[4,512,384]{2,1,0:T(8,128)(2,1)} async-done(((bf16[4,512,384]{2,1,0:T(8,128)(2,1)}), bf16[4,512,384]{2,1,0:T(8,128)(2,1)}, u32[]{:S(2)}, u32[]{:S(2)}) %all-to-all-start) | async-done | bytes 1572896 | tf_op jit(solution)/shard_map/all_to_all | solution.py:66
  120.9 7.5 %shard_map.333 = (bf16[4,4,2,64,128]{4,3,2,1,0:T(8,128)(2,1)S(1)}, f32[2,1024,128]{2,1,0:T(8,128)S(1)}, f32[2,1024,128]{2,1,0:T(8,128)S(1)}) custom-call(s32[3]{0:T(128)S(1)} %pad_add_fusion.live_ref, bf16[4,4,2,64,384]{4,3,2,1,0:T(8,128)(2,1)} %bitcast.13.qkv_ref), custom_call_target="tpu_custom_call" | custom-call | flops 4000000000 | bytes 4194304 | tf_op jit(solution)/shard_map/pallas_call | solution.py:413
  128.4 10.0 %all_to_all.45.heads_ref.grad_ref = bf16[4,512,128]{2,1,0:T(8,128)(2,1)} all-to-all(bf16[4,512,128]{2,1,0:T(8,128)(2,1)S(1)} %bitcast.77), channel_id=1, replica_groups=mesh['z'=4,'c'=2,'x'=4,'y'=4] {'x'}, dimensions={0} | all-to-all | bytes 1048576 | tf_op jit(solution)/shard_map/all_to_all | solution.py:66
  138.9 5.9 %shard_map.334 = bf16[512,2048]{1,0:T(8,128)(2,1)} custom-call(s32[4]{0:T(128)} %iota.9.place_ref, bf16[4,512,128]{2,1,0:T(8,128)(2,1)} %all_to_all.45.heads_ref.grad_ref, bf16[8,4,256,512]{3,2,1,0:T(8,128)(2,1)} %bitcast.81), custom_call_target="tpu_custom_call" | custom-call | flops 1073741824 | bytes 5242880 | tf_op jit(solution)/shard_map/pallas_call | solution.py:175
  149.1 4.1 collective-permute-done.15
  155.2 6.2 %collective-permute-done.16 = bf16[64,2048]{1,0:T(8,128)(2,1)S(1)} collective-permute-done((bf16[64,2048]{1,0:T(8,128)(2,1)S(1)}, bf16[64,2048]{1,0:T(8,128)(2,1)S(1)}, u32[]{:S(2)}, u32[]{:S(2)}) %collective-permute-start.16) | collective-permute-done | bytes 262176 | tf_op jit(solution)/shard_map/ppermute | solution.py:72
  161.6 4.2 collective-permute-done.18
  170.4 3.1 collective-permute-start.24
  175.3 2.7 collective-permute-start.23
  179.2 3.0 collective-permute-start.26
  185.7 3.5 collective-permute-done.25
  190.6 21.4 %shard_map.335 = (bf16[512,2048]{1,0:T(8,128)(2,1)}, bf16[512,2048]{1,0:T(8,128)(2,1)}, bf16[512,2048]{1,0:T(8,128)(2,1)}, f32[4,1,512]{2,1,0:T(1,128)}) custom-call(s32[4]{0:T(128)} %get-tuple-element.176.place_ref, bf16[512,2048]{1,0:T(8,128)(2,1)} %constant_dynamic-update-slice_fusion.14.norm_ref, ...), custom_call_target="tpu_custom_call" | custom-call | flops 12884901888 | bytes 26214400 | tf_op jit(solution)/shard_map/pallas_call | solution.py:275
  212.0 4.5 %all-to-all-start.2 = ((bf16[4,128,2048]{2,1,0:T(8,128)(2,1)}), bf16[4,128,2048]{2,1,0:T(8,128)(2,1)}, u32[]{:S(2)}, u32[]{:S(2)}) async-start(bf16[4,128,2048]{2,1,0:T(8,128)(2,1)} %bitcast.87), calls=%async_computation.2 | async-start | bytes 4194304 | tf_op jit(solution)/shard_map/all_to_all | solution.py:66
  216.6 22.2 %shard_map.336 = (bf16[512,2048]{1,0:T(8,128)(2,1)}, bf16[8,4,256,1024]{3,2,1,0:T(8,128)(2,1)}) custom-call(s32[4]{0:T(128)} %get-tuple-element.114.place_ref, bf16[512,2048]{1,0:T(8,128)(2,1)} %constant_dynamic-update-slice_fusion.14.norm_ref, bf16[512,2048]{1,0:T(8,128)(2,1)} %constant_dynamic-update-slice_fusion.7.cot_ref, ...), custom_call_target="tpu_custom_call" | custom-call | flops 12884901888 | bytes 41943040 | tf_op jit(solution)/shard_map/pallas_call | solution.py:323
  239.0 3.5 shard_map.337
  248.7 2.9 collective-permute-start.32
  259.4 5.8 %shard_map.338 = bf16[4,512,128]{2,1,0:T(8,128)(2,1)} custom-call(bf16[512,2048]{1,0:T(8,128)(2,1)} %constant_dynamic-update-slice_fusion.21.rows_ref, bf16[8,4,256,512]{3,2,1,0:T(8,128)(2,1)} %bitcast.82), custom_call_target="tpu_custom_call" | custom-call | flops 1073741824 | bytes 5242880 | tf_op jit(solution)/shard_map/pallas_call | solution.py:199
  265.3 10.5 %all_to_all.46 = bf16[4,512,128]{2,1,0:T(8,128)(2,1)S(1)} all-to-all(bf16[4,512,128]{2,1,0:T(8,128)(2,1)} %shard_map.338), channel_id=1, replica_groups=mesh['z'=4,'c'=2,'x'=4,'y'=4] {'x'}, dimensions={0} | all-to-all | bytes 1048576 | tf_op jit(solution)/shard_map/all_to_all | solution.py:66
  278.3 11.8 %shard_map.339 = (bf16[4,4,2,64,384]{4,3,2,1,0:T(8,128)(2,1)}, f32[2,1,384]{2,1,0:T(1,128)S(1)}) custom-call(s32[3]{0:T(128)S(1)} %pad_add_fusion.live_ref, bf16[4,4,2,64,384]{4,3,2,1,0:T(8,128)(2,1)} %bitcast.13.qkv_ref, bf16[4,4,2,64,128]{4,3,2,1,0:T(8,128)(2,1)S(1)} %bitcast.76, f32[2,1024,128]{2,1,0:T(8,128)S(1)} %copy-done.5, f32[2,1024,128]{2,1,0:T(8,128)S(1)} %copy-done.7), custom_call_target="tpu_custom_call" | custom-call | flops 8000000000 | bytes 8388608 | tf_op jit(solution)/shard_map/pallas_call | solution.py:490
  290.0 4.3 all-to-all-start.4
  298.5 6.1 %shard_map.340.refs_0_ = bf16[8,4,256,512]{3,2,1,0:T(8,128)(2,1)} custom-call(bf16[512,2048]{1,0:T(8,128)(2,1)} %constant_dynamic-update-slice_fusion.21.rows_ref, bf16[4,512,128]{2,1,0:T(8,128)(2,1)} %all_to_all.45.heads_ref.grad_ref), custom_call_target="tpu_custom_call" | custom-call | flops 1073741824 | bytes 15728640 | tf_op jit(solution)/shard_map/pallas_call | solution.py:224
  307.0 5.8 %collective-permute-done.34 = bf16[128,2048]{1,0:T(8,128)(2,1)} collective-permute-done((bf16[128,2048]{1,0:T(8,128)(2,1)}, bf16[128,2048]{1,0:T(8,128)(2,1)}, u32[]{:S(2)}, u32[]{:S(2)}) %collective-permute-start.34) | collective-permute-done | bytes 524320 | tf_op jit(solution)/shard_map/ppermute | solution.py:72
  312.8 2.7 add_convert_fusion
  315.5 8.3 %shard_map.341 = bf16[8,4,256,512]{3,2,1,0:T(8,128)(2,1)} custom-call(bf16[512,2048]{1,0:T(8,128)(2,1)} %copy-done.8, bf16[4,512,384]{2,1,0:T(8,128)(2,1)} %all-to-all-done.4.grad_ref.heads_ref, bf16[8,4,256,512]{3,2,1,0:T(8,128)(2,1)} %shard_map.340.refs_0_), custom_call_target="tpu_custom_call", output_to_operand_aliasing={{}: (2, {})} | custom-call | flops 3221225472 | bytes 15728640 | tf_op jit(solution)/shard_map/pallas_call | solution.py:224
  323.7 20.7 %reduce-scatter.3.cloned.1.call-done = bf16[1,4,256,1024]{3,2,1,0:T(8,128)(2,1)} async-done(((bf16[8,4,256,1024]{3,2,1,0:T(8,128)(2,1)}), bf16[1,4,256,1024]{3,2,1,0:T(8,128)(2,1)}) %reduce-scatter.3.cloned.1.call-update) | async-done | bytes 2097168 | tf_op jit(solution)/shard_map/reduce_scatter | solution.py:127
  353.8 4.6 %all-to-all-start.5 = ((bf16[4,256,1024]{2,1,0:T(8,128)(2,1)}), bf16[4,256,1024]{2,1,0:T(8,128)(2,1)}, u32[]{:S(2)}, u32[]{:S(2)}) async-start(bf16[4,256,1024]{2,1,0:T(8,128)(2,1)} %bitcast.86), calls=%async_computation.6 | async-start | bytes 4194304 | tf_op jit(solution)/shard_map/all_to_all | solution.py:66
  358.9 9.1 %shard_map.342 = bf16[512,2048]{1,0:T(8,128)(2,1)} custom-call(s32[4]{0:T(128)} %iota.10.place_ref, bf16[4,512,384]{2,1,0:T(8,128)(2,1)} %all-to-all-done.4.grad_ref.heads_ref, bf16[8,4,256,512]{3,2,1,0:T(8,128)(2,1)} %bitcast.83), custom_call_target="tpu_custom_call" | custom-call | flops 3221225472 | bytes 5242880 | tf_op jit(solution)/shard_map/pallas_call | solution.py:175
  372.5 3.0 collective-permute-start.39
  376.8 3.2 collective-permute-done.36
  387.9 2.7 collective-permute-done.37.refs_1_
  393.9 4.3 all-to-all-start.6
  400.4 4.5 %all-to-all-done.6 = f32[16,12,128]{2,1,0:T(8,128)S(1)} async-done(((f32[16,12,128]{2,1,0:T(8,128)}), f32[16,12,128]{2,1,0:T(8,128)S(1)}, u32[]{:S(2)}, u32[]{:S(2)}) %all-to-all-start.6) | async-done | bytes 98336 | tf_op jit(solution)/shard_map/all_to_all | solution.py:62
  405.6 9.0 %all-to-all-start.7 = ((f32[8,12,128]{2,1,0:T(8,128)}), f32[8,12,128]{2,1,0:T(8,128)S(1)}, u32[]{:S(2)}, u32[]{:S(2)}) async-start(f32[8,12,128]{2,1,0:T(8,128)} %broadcast_in_dim.19), calls=%async_computation.9 | async-start | bytes 131072 | tf_op jit(solution)/shard_map/all_to_all | solution.py:58
  420.2 3.8 all-to-all-start.8
  425.0 9.0 %all-to-all-done.8 = f32[16,12,128]{2,1,0:T(8,128)S(1)} async-done(((f32[16,12,128]{2,1,0:T(8,128)}), f32[16,12,128]{2,1,0:T(8,128)S(1)}, u32[]{:S(2)}, u32[]{:S(2)}) %all-to-all-start.8) | async-done | bytes 98336 | tf_op jit(solution)/shard_map/all_to_all | solution.py:58
  (263 shorter events, 99.2 us)
Async XLA Ops:
  7.2 83.0 %all-gather.4.cloned.1.call-start = ((), (), s32[]{:S(2)}) async-start(), calls=%async_computation.11 | async-start | bytes 8650752 | tf_op jit(solution)/shard_map/all_gather | solution.py:122
  10.1 180.6 %all-gather.6.cloned.1.call-start = ((), (), s32[]{:S(2)}) async-start(), calls=%async_computation.14 | async-start | bytes 18874368 | tf_op jit(solution)/shard_map/all_gather | solution.py:636
  13.0 8.9 %collective-permute-start.3 = (bf16[64,2048]{1,0:T(8,128)(2,1)}, bf16[64,2048]{1,0:T(8,128)(2,1)S(1)}, u32[]{:S(2)}, u32[]{:S(2)}) collective-permute-start(bf16[64,2048]{1,0:T(8,128)(2,1)} %get-tuple-element.151), channel_id=1, source_target_pairs={{0,3},{1,0},{2,1},{3,2},{4,7},{5,4},{6,5},{7,6},{8,11},{9,8},{10,9... | collective-permute-start | bytes 786440 | tf_op jit(solution)/shard_map/ppermute | solution.py:72
  16.6 15.0 %collective-permute-start.1 = (bf16[64,2048]{1,0:T(8,128)(2,1)}, bf16[64,2048]{1,0:T(8,128)(2,1)}, u32[]{:S(2)}, u32[]{:S(2)}) collective-permute-start(bf16[64,2048]{1,0:T(8,128)(2,1)} %get-tuple-element.151), channel_id=1, source_target_pairs={{0,1},{1,2},{2,3},{3,0},{4,5},{5,6},{6,7},{7,4},{8,9},{9,10},{10,1... | collective-permute-start | bytes 786440 | tf_op jit(solution)/shard_map/ppermute | solution.py:72
  16.6 16.0 %collective-permute-start.2 = (bf16[64,2048]{1,0:T(8,128)(2,1)}, bf16[64,2048]{1,0:T(8,128)(2,1)}, u32[]{:S(2)}, u32[]{:S(2)}) collective-permute-start(bf16[64,2048]{1,0:T(8,128)(2,1)} %get-tuple-element.152), channel_id=1, source_target_pairs={{0,3},{1,0},{2,1},{3,2},{4,7},{5,4},{6,5},{7,6},{8,11},{9,8},{10,9... | collective-permute-start | bytes 786440 | tf_op jit(solution)/shard_map/ppermute | solution.py:72
  19.2 11.3 %collective-permute-start = (bf16[64,2048]{1,0:T(8,128)(2,1)}, bf16[64,2048]{1,0:T(8,128)(2,1)}, u32[]{:S(2)}, u32[]{:S(2)}) collective-permute-start(bf16[64,2048]{1,0:T(8,128)(2,1)} %get-tuple-element.152), channel_id=1, source_target_pairs={{0,1},{1,2},{2,3},{3,0},{4,5},{5,6},{6,7},{7,4},{8,9},{9,10},{10,1... | collective-permute-start | bytes 786440 | tf_op jit(solution)/shard_map/ppermute | solution.py:72
  21.8 16.1 %collective-permute-start.5 = (bf16[64,2048]{1,0:T(8,128)(2,1)S(1)}, bf16[64,2048]{1,0:T(8,128)(2,1)S(1)}, u32[]{:S(2)}, u32[]{:S(2)}) collective-permute-start(bf16[64,2048]{1,0:T(8,128)(2,1)S(1)} %collective-permute-done.3), channel_id=1, source_target_pairs={{0,3},{1,0},{2,1},{3,2},{4,7},{5,4},{6,5},{7,6},{8,11},{9,8},{10,9... | collective-permute-start | bytes 786440 | tf_op jit(solution)/shard_map/ppermute | solution.py:72
  30.6 7.4 %collective-permute-start.4 = (bf16[64,2048]{1,0:T(8,128)(2,1)}, bf16[64,2048]{1,0:T(8,128)(2,1)S(1)}, u32[]{:S(2)}, u32[]{:S(2)}) collective-permute-start(bf16[64,2048]{1,0:T(8,128)(2,1)} %collective-permute-done), channel_id=1, source_target_pairs={{0,1},{1,2},{2,3},{3,0},{4,5},{5,6},{6,7},{7,4},{8,9},{9,10},{10,1... | collective-permute-start | bytes 786440 | tf_op jit(solution)/shard_map/ppermute | solution.py:72
  38.0 15.5 %collective-permute-start.10 = (bf16[256,1024]{1,0:T(8,128)(2,1)S(1)}, bf16[256,1024]{1,0:T(8,128)(2,1)S(1)}, u32[]{:S(2)}, u32[]{:S(2)}) collective-permute-start(bf16[256,1024]{1,0:T(8,128)(2,1)S(1)} %pad_maximum_fusion.2), channel_id=1, source_target_pairs={{0,8},{4,12},{8,0},{12,4},{1,9},{5,13},{9,1},{13,5},{2,10},{6,14},... | collective-permute-start | bytes 1572872 | tf_op jit(solution)/shard_map/ppermute | solution.py:72
  40.8 34.3 %collective-permute-start.9 = (bf16[256,1024]{1,0:T(8,128)(2,1)S(1)}, bf16[256,1024]{1,0:T(8,128)(2,1)S(1)}, u32[]{:S(2)}, u32[]{:S(2)}) collective-permute-start(bf16[256,1024]{1,0:T(8,128)(2,1)S(1)} %pad_maximum_fusion.2), channel_id=1, source_target_pairs={{0,12},{4,0},{8,4},{12,8},{1,13},{5,1},{9,5},{13,9},{2,14},{6,2},{... | collective-permute-start | bytes 1572872 | tf_op jit(solution)/shard_map/ppermute | solution.py:72
  41.7 34.1 %collective-permute-start.8 = (bf16[256,1024]{1,0:T(8,128)(2,1)S(1)}, bf16[256,1024]{1,0:T(8,128)(2,1)S(1)}, u32[]{:S(2)}, u32[]{:S(2)}) collective-permute-start(bf16[256,1024]{1,0:T(8,128)(2,1)S(1)} %pad_maximum_fusion.2), channel_id=1, source_target_pairs={{0,4},{4,8},{8,12},{12,0},{1,5},{5,9},{9,13},{13,1},{2,6},{6,10},{... | collective-permute-start | bytes 1572872 | tf_op jit(solution)/shard_map/ppermute | solution.py:72
  42.4 6.9 %collective-permute-start.6 = (bf16[64,2048]{1,0:T(8,128)(2,1)S(1)}, bf16[64,2048]{1,0:T(8,128)(2,1)S(1)}, u32[]{:S(2)}, u32[]{:S(2)}) collective-permute-start(bf16[64,2048]{1,0:T(8,128)(2,1)S(1)} %get-tuple-element.150), channel_id=1, source_target_pairs={{0,1},{1,2},{2,3},{3,0},{4,5},{5,6},{6,7},{7,4},{8,9},{9,10},{10,1... | collective-permute-start | bytes 786440 | tf_op jit(solution)/shard_map/ppermute | solution.py:72
  78.9 6.9 %collective-permute-start.11 = (bf16[64,2048]{1,0:T(8,128)(2,1)S(1)}, bf16[64,2048]{1,0:T(8,128)(2,1)S(1)}, u32[]{:S(2)}, u32[]{:S(2)}) collective-permute-start(bf16[64,2048]{1,0:T(8,128)(2,1)S(1)} %copy-done.19), channel_id=1, source_target_pairs={{0,1},{1,2},{2,3},{3,0},{4,5},{5,6},{6,7},{7,4},{8,9},{9,10},{10,1... | collective-permute-start | bytes 786440 | tf_op jit(solution)/shard_map/ppermute | solution.py:72
  78.9 7.6 %collective-permute-start.12 = (bf16[64,2048]{1,0:T(8,128)(2,1)S(1)}, bf16[64,2048]{1,0:T(8,128)(2,1)S(1)}, u32[]{:S(2)}, u32[]{:S(2)}) collective-permute-start(bf16[64,2048]{1,0:T(8,128)(2,1)S(1)} %copy-done.17), channel_id=1, source_target_pairs={{0,3},{1,0},{2,1},{3,2},{4,7},{5,4},{6,5},{7,6},{8,11},{9,8},{10,9... | collective-permute-start | bytes 786440 | tf_op jit(solution)/shard_map/ppermute | solution.py:72
  82.4 7.1 %collective-permute-start.14 = (bf16[64,2048]{1,0:T(8,128)(2,1)S(1)}, bf16[64,2048]{1,0:T(8,128)(2,1)S(1)}, u32[]{:S(2)}, u32[]{:S(2)}) collective-permute-start(bf16[64,2048]{1,0:T(8,128)(2,1)S(1)} %collective-permute-done.7), channel_id=1, source_target_pairs={{0,3},{1,0},{2,1},{3,2},{4,7},{5,4},{6,5},{7,6},{8,11},{9,8},{10,9... | collective-permute-start | bytes 786440 | tf_op jit(solution)/shard_map/ppermute | solution.py:72
  98.9 22.0 %all-to-all-start = ((bf16[4,512,384]{2,1,0:T(8,128)(2,1)}), bf16[4,512,384]{2,1,0:T(8,128)(2,1)}, u32[]{:S(2)}, u32[]{:S(2)}) async-start(bf16[4,512,384]{2,1,0:T(8,128)(2,1)} %shard_map.332), calls=%async_computation | async-start | bytes 3145728 | tf_op jit(solution)/shard_map/all_to_all | solution.py:66
  146.3 6.9 %collective-permute-start.15 = (bf16[64,2048]{1,0:T(8,128)(2,1)S(1)}, bf16[64,2048]{1,0:T(8,128)(2,1)S(1)}, u32[]{:S(2)}, u32[]{:S(2)}) collective-permute-start(bf16[64,2048]{1,0:T(8,128)(2,1)S(1)} %get-tuple-element.130), channel_id=1, source_target_pairs={{0,1},{1,2},{2,3},{3,0},{4,5},{5,6},{6,7},{7,4},{8,9},{9,10},{10,1... | collective-permute-start | bytes 786440 | tf_op jit(solution)/shard_map/ppermute | solution.py:72
  146.4 7.1 %collective-permute-start.19 = (bf16[64,2048]{1,0:T(8,128)(2,1)S(1)}, bf16[64,2048]{1,0:T(8,128)(2,1)S(1)}, u32[]{:S(2)}, u32[]{:S(2)}) collective-permute-start(bf16[64,2048]{1,0:T(8,128)(2,1)S(1)} %get-tuple-element.131), channel_id=1, source_target_pairs={{0,3},{1,0},{2,1},{3,2},{4,7},{5,4},{6,5},{7,6},{8,11},{9,8},{10,9... | collective-permute-start | bytes 786440 | tf_op jit(solution)/shard_map/ppermute | solution.py:72
  153.3 8.1 %collective-permute-start.16 = (bf16[64,2048]{1,0:T(8,128)(2,1)S(1)}, bf16[64,2048]{1,0:T(8,128)(2,1)S(1)}, u32[]{:S(2)}, u32[]{:S(2)}) collective-permute-start(bf16[64,2048]{1,0:T(8,128)(2,1)S(1)} %add_convert_fusion.5), channel_id=1, source_target_pairs={{0,1},{1,2},{2,3},{3,0},{4,5},{5,6},{6,7},{7,4},{8,9},{9,10},{10,1... | collective-permute-start | bytes 786440 | tf_op jit(solution)/shard_map/ppermute | solution.py:72
  153.3 12.4 %collective-permute-start.18 = (bf16[64,2048]{1,0:T(8,128)(2,1)S(1)}, bf16[64,2048]{1,0:T(8,128)(2,1)S(1)}, u32[]{:S(2)}, u32[]{:S(2)}) collective-permute-start(bf16[64,2048]{1,0:T(8,128)(2,1)S(1)} %get-tuple-element.132), channel_id=1, source_target_pairs={{0,1},{1,2},{2,3},{3,0},{4,5},{5,6},{6,7},{7,4},{8,9},{9,10},{10,1... | collective-permute-start | bytes 786440 | tf_op jit(solution)/shard_map/ppermute | solution.py:72
  170.4 8.8 %collective-permute-start.24 = (bf16[64,2048]{1,0:T(8,128)(2,1)}, bf16[64,2048]{1,0:T(8,128)(2,1)S(1)}, u32[]{:S(2)}, u32[]{:S(2)}) collective-permute-start(bf16[64,2048]{1,0:T(8,128)(2,1)} %get-tuple-element.147), channel_id=1, source_target_pairs={{0,3},{1,0},{2,1},{3,2},{4,7},{5,4},{6,5},{7,6},{8,11},{9,8},{10,9... | collective-permute-start | bytes 786440 | tf_op jit(solution)/shard_map/ppermute | solution.py:72
  173.5 8.8 %collective-permute-start.21 = (bf16[64,2048]{1,0:T(8,128)(2,1)S(1)}, bf16[64,2048]{1,0:T(8,128)(2,1)S(1)}, u32[]{:S(2)}, u32[]{:S(2)}) collective-permute-start(bf16[64,2048]{1,0:T(8,128)(2,1)S(1)} %get-tuple-element.148), channel_id=1, source_target_pairs={{0,1},{1,2},{2,3},{3,0},{4,5},{5,6},{6,7},{7,4},{8,9},{9,10},{10,1... | collective-permute-start | bytes 786440 | tf_op jit(solution)/shard_map/ppermute | solution.py:72
  174.0 9.5 %collective-permute-start.22 = (bf16[64,2048]{1,0:T(8,128)(2,1)}, bf16[64,2048]{1,0:T(8,128)(2,1)S(1)}, u32[]{:S(2)}, u32[]{:S(2)}) collective-permute-start(bf16[64,2048]{1,0:T(8,128)(2,1)} %get-tuple-element.147), channel_id=1, source_target_pairs={{0,1},{1,2},{2,3},{3,0},{4,5},{5,6},{6,7},{7,4},{8,9},{9,10},{10,1... | collective-permute-start | bytes 786440 | tf_op jit(solution)/shard_map/ppermute | solution.py:72
  175.3 8.9 %collective-permute-start.23 = (bf16[64,2048]{1,0:T(8,128)(2,1)S(1)}, bf16[64,2048]{1,0:T(8,128)(2,1)S(1)}, u32[]{:S(2)}, u32[]{:S(2)}) collective-permute-start(bf16[64,2048]{1,0:T(8,128)(2,1)S(1)} %get-tuple-element.148), channel_id=1, source_target_pairs={{0,3},{1,0},{2,1},{3,2},{4,7},{5,4},{6,5},{7,6},{8,11},{9,8},{10,9... | collective-permute-start | bytes 786440 | tf_op jit(solution)/shard_map/ppermute | solution.py:72
  179.2 10.7 %collective-permute-start.26 = (bf16[64,2048]{1,0:T(8,128)(2,1)S(1)}, bf16[64,2048]{1,0:T(8,128)(2,1)S(1)}, u32[]{:S(2)}, u32[]{:S(2)}) collective-permute-start(bf16[64,2048]{1,0:T(8,128)(2,1)S(1)} %collective-permute-done.24), channel_id=1, source_target_pairs={{0,3},{1,0},{2,1},{3,2},{4,7},{5,4},{6,5},{7,6},{8,11},{9,8},{10,9... | collective-permute-start | bytes 786440 | tf_op jit(solution)/shard_map/ppermute | solution.py:72
  182.2 6.9 %collective-permute-start.25 = (bf16[64,2048]{1,0:T(8,128)(2,1)S(1)}, bf16[64,2048]{1,0:T(8,128)(2,1)S(1)}, u32[]{:S(2)}, u32[]{:S(2)}) collective-permute-start(bf16[64,2048]{1,0:T(8,128)(2,1)S(1)} %collective-permute-done.21), channel_id=1, source_target_pairs={{0,1},{1,2},{2,3},{3,0},{4,5},{5,6},{6,7},{7,4},{8,9},{9,10},{10,1... | collective-permute-start | bytes 786440 | tf_op jit(solution)/shard_map/ppermute | solution.py:72
  212.0 26.8 %all-to-all-start.2 = ((bf16[4,128,2048]{2,1,0:T(8,128)(2,1)}), bf16[4,128,2048]{2,1,0:T(8,128)(2,1)}, u32[]{:S(2)}, u32[]{:S(2)}) async-start(bf16[4,128,2048]{2,1,0:T(8,128)(2,1)} %bitcast.87), calls=%async_computation.2 | async-start | bytes 4194304 | tf_op jit(solution)/shard_map/all_to_all | solution.py:66
  216.5 127.9 %reduce-scatter.3.cloned.1.call-start = ((), (), s32[]{:S(2)}) async-start(), calls=%async_computation.12 | async-start | bytes 18874368 | tf_op jit(solution)/shard_map/reduce_scatter | solution.py:127
  245.2 9.2 %collective-permute-start.28 = (bf16[64,2048]{1,0:T(8,128)(2,1)S(1)}, bf16[64,2048]{1,0:T(8,128)(2,1)S(1)}, u32[]{:S(2)}, u32[]{:S(2)}) collective-permute-start(bf16[64,2048]{1,0:T(8,128)(2,1)S(1)} %get-tuple-element.145), channel_id=1, source_target_pairs={{0,1},{1,2},{2,3},{3,0},{4,5},{5,6},{6,7},{7,4},{8,9},{9,10},{10,1... | collective-permute-start | bytes 786440 | tf_op jit(solution)/shard_map/ppermute | solution.py:72
  245.4 9.7 %collective-permute-start.29 = (bf16[64,2048]{1,0:T(8,128)(2,1)S(1)}, bf16[64,2048]{1,0:T(8,128)(2,1)S(1)}, u32[]{:S(2)}, u32[]{:S(2)}) collective-permute-start(bf16[64,2048]{1,0:T(8,128)(2,1)S(1)} %get-tuple-element.146), channel_id=1, source_target_pairs={{0,3},{1,0},{2,1},{3,2},{4,7},{5,4},{6,5},{7,6},{8,11},{9,8},{10,9... | collective-permute-start | bytes 786440 | tf_op jit(solution)/shard_map/ppermute | solution.py:72
  248.7 10.0 %collective-permute-start.32 = (bf16[64,2048]{1,0:T(8,128)(2,1)S(1)}, bf16[64,2048]{1,0:T(8,128)(2,1)S(1)}, u32[]{:S(2)}, u32[]{:S(2)}) collective-permute-start(bf16[64,2048]{1,0:T(8,128)(2,1)S(1)} %collective-permute-done.30), channel_id=1, source_target_pairs={{0,3},{1,0},{2,1},{3,2},{4,7},{5,4},{6,5},{7,6},{8,11},{9,8},{10,9... | collective-permute-start | bytes 786440 | tf_op jit(solution)/shard_map/ppermute | solution.py:72
  290.0 25.4 %all-to-all-start.4 = ((bf16[4,512,384]{2,1,0:T(8,128)(2,1)}), bf16[4,512,384]{2,1,0:T(8,128)(2,1)}, u32[]{:S(2)}, u32[]{:S(2)}) async-start(bf16[4,512,384]{2,1,0:T(8,128)(2,1)} %bitcast.24), calls=%async_computation.4 | async-start | bytes 3145728 | tf_op jit(solution)/shard_map/all_to_all | solution.py:66
  294.4 110.6 %reduce-scatter.5.cloned.1.call-start = ((), (), s32[]{:S(2)}) async-start(), calls=%async_computation.13 | async-start | bytes 9437184 | tf_op jit(solution)/shard_map/reduce_scatter | solution.py:127
  297.0 8.6 %collective-permute-start.33 = (bf16[128,2048]{1,0:T(8,128)(2,1)}, bf16[128,2048]{1,0:T(8,128)(2,1)S(1)}, u32[]{:S(2)}, u32[]{:S(2)}) collective-permute-start(bf16[128,2048]{1,0:T(8,128)(2,1)} %get-tuple-element.125), channel_id=1, source_target_pairs={{0,3},{1,0},{2,1},{3,2},{4,7},{5,4},{6,5},{7,6},{8,11},{9,8},{10,9... | collective-permute-start | bytes 1572872 | tf_op jit(solution)/shard_map/ppermute | solution.py:72
  297.0 10.0 %collective-permute-start.35 = (bf16[128,2048]{1,0:T(8,128)(2,1)}, bf16[128,2048]{1,0:T(8,128)(2,1)}, u32[]{:S(2)}, u32[]{:S(2)}) collective-permute-start(bf16[128,2048]{1,0:T(8,128)(2,1)} %get-tuple-element.126), channel_id=1, source_target_pairs={{0,2},{1,3},{2,0},{3,1},{4,6},{5,7},{6,4},{7,5},{8,10},{9,11},{10,... | collective-permute-start | bytes 1572872 | tf_op jit(solution)/shard_map/ppermute | solution.py:72
  297.6 15.2 %collective-permute-start.34 = (bf16[128,2048]{1,0:T(8,128)(2,1)}, bf16[128,2048]{1,0:T(8,128)(2,1)}, u32[]{:S(2)}, u32[]{:S(2)}) collective-permute-start(bf16[128,2048]{1,0:T(8,128)(2,1)} %get-tuple-element.127), channel_id=1, source_target_pairs={{0,1},{1,2},{2,3},{3,0},{4,5},{5,6},{6,7},{7,4},{8,9},{9,10},{10,1... | collective-permute-start | bytes 1572872 | tf_op jit(solution)/shard_map/ppermute | solution.py:72
  353.8 36.8 %all-to-all-start.5 = ((bf16[4,256,1024]{2,1,0:T(8,128)(2,1)}), bf16[4,256,1024]{2,1,0:T(8,128)(2,1)}, u32[]{:S(2)}, u32[]{:S(2)}) async-start(bf16[4,256,1024]{2,1,0:T(8,128)(2,1)} %bitcast.86), calls=%async_computation.6 | async-start | bytes 4194304 | tf_op jit(solution)/shard_map/all_to_all | solution.py:66
  370.1 6.8 %collective-permute-start.40 = (bf16[64,2048]{1,0:T(8,128)(2,1)S(1)}, bf16[64,2048]{1,0:T(8,128)(2,1)S(1)}, u32[]{:S(2)}, u32[]{:S(2)}) collective-permute-start(bf16[64,2048]{1,0:T(8,128)(2,1)S(1)} %get-tuple-element.121), channel_id=1, source_target_pairs={{0,3},{1,0},{2,1},{3,2},{4,7},{5,4},{6,5},{7,6},{8,11},{9,8},{10,9... | collective-permute-start | bytes 786440 | tf_op jit(solution)/shard_map/ppermute | solution.py:72
  372.5 7.5 %collective-permute-start.36 = (bf16[64,2048]{1,0:T(8,128)(2,1)S(1)}, bf16[64,2048]{1,0:T(8,128)(2,1)S(1)}, u32[]{:S(2)}, u32[]{:S(2)}) collective-permute-start(bf16[64,2048]{1,0:T(8,128)(2,1)S(1)} %get-tuple-element.124), channel_id=1, source_target_pairs={{0,1},{1,2},{2,3},{3,0},{4,5},{5,6},{6,7},{7,4},{8,9},{9,10},{10,1... | collective-permute-start | bytes 786440 | tf_op jit(solution)/shard_map/ppermute | solution.py:72
  372.5 12.2 %collective-permute-start.39 = (bf16[64,2048]{1,0:T(8,128)(2,1)}, bf16[64,2048]{1,0:T(8,128)(2,1)S(1)}, u32[]{:S(2)}, u32[]{:S(2)}) collective-permute-start(bf16[64,2048]{1,0:T(8,128)(2,1)} %get-tuple-element.122), channel_id=1, source_target_pairs={{0,3},{1,0},{2,1},{3,2},{4,7},{5,4},{6,5},{7,6},{8,11},{9,8},{10,9... | collective-permute-start | bytes 786440 | tf_op jit(solution)/shard_map/ppermute | solution.py:72
  375.5 10.2 %collective-permute-start.38 = (bf16[64,2048]{1,0:T(8,128)(2,1)}, bf16[64,2048]{1,0:T(8,128)(2,1)S(1)}, u32[]{:S(2)}, u32[]{:S(2)}) collective-permute-start(bf16[64,2048]{1,0:T(8,128)(2,1)} %get-tuple-element.123), channel_id=1, source_target_pairs={{0,1},{1,2},{2,3},{3,0},{4,5},{5,6},{6,7},{7,4},{8,9},{9,10},{10,1... | collective-permute-start | bytes 786440 | tf_op jit(solution)/shard_map/ppermute | solution.py:72
  382.4 8.2 %collective-permute-start.37 = (bf16[64,2048]{1,0:T(8,128)(2,1)}, bf16[64,2048]{1,0:T(8,128)(2,1)S(1)}, u32[]{:S(2)}, u32[]{:S(2)}) collective-permute-start(bf16[64,2048]{1,0:T(8,128)(2,1)} %get-tuple-element.120), channel_id=1, source_target_pairs={{0,1},{1,2},{2,3},{3,0},{4,5},{5,6},{6,7},{7,4},{8,9},{9,10},{10,1... | collective-permute-start | bytes 786440 | tf_op jit(solution)/shard_map/ppermute | solution.py:72
  393.9 11.0 %all-to-all-start.6 = ((f32[16,12,128]{2,1,0:T(8,128)}), f32[16,12,128]{2,1,0:T(8,128)S(1)}, u32[]{:S(2)}, u32[]{:S(2)}) async-start(f32[16,12,128]{2,1,0:T(8,128)} %reshape.307), calls=%async_computation.7 | async-start | bytes 262144 | tf_op jit(solution)/shard_map/all_to_all | solution.py:62
  405.6 13.9 %all-to-all-start.7 = ((f32[8,12,128]{2,1,0:T(8,128)}), f32[8,12,128]{2,1,0:T(8,128)S(1)}, u32[]{:S(2)}, u32[]{:S(2)}) async-start(f32[8,12,128]{2,1,0:T(8,128)} %broadcast_in_dim.19), calls=%async_computation.9 | async-start | bytes 131072 | tf_op jit(solution)/shard_map/all_to_all | solution.py:58
  415.8 19.5 %collective-permute-start.42 = (bf16[256,512]{1,0:T(8,128)(2,1)S(1)}, bf16[256,512]{1,0:T(8,128)(2,1)S(1)}, u32[]{:S(2)}, u32[]{:S(2)}) collective-permute-start(bf16[256,512]{1,0:T(8,128)(2,1)S(1)} %get-tuple-element.136), channel_id=1, source_target_pairs={{0,12},{4,0},{8,4},{12,8},{1,13},{5,1},{9,5},{13,9},{2,14},{6,2},{... | collective-permute-start | bytes 786440 | tf_op jit(solution)/shard_map/ppermute | solution.py:72
  416.7 18.5 %collective-permute-start.44 = (bf16[256,512]{1,0:T(8,128)(2,1)S(1)}, bf16[256,512]{1,0:T(8,128)(2,1)S(1)}, u32[]{:S(2)}, u32[]{:S(2)}) collective-permute-start(bf16[256,512]{1,0:T(8,128)(2,1)S(1)} %get-tuple-element.137), channel_id=1, source_target_pairs={{0,8},{4,12},{8,0},{12,4},{1,9},{5,13},{9,1},{13,5},{2,10},{6,14},... | collective-permute-start | bytes 786440 | tf_op jit(solution)/shard_map/ppermute | solution.py:72
  417.8 17.4 %collective-permute-start.43 = (bf16[256,512]{1,0:T(8,128)(2,1)S(1)}, bf16[256,512]{1,0:T(8,128)(2,1)S(1)}, u32[]{:S(2)}, u32[]{:S(2)}) collective-permute-start(bf16[256,512]{1,0:T(8,128)(2,1)S(1)} %get-tuple-element.138), channel_id=1, source_target_pairs={{0,4},{4,8},{8,12},{12,0},{1,5},{5,9},{9,13},{13,1},{2,6},{6,10},{... | collective-permute-start | bytes 786440 | tf_op jit(solution)/shard_map/ppermute | solution.py:72
  420.2 13.8 %all-to-all-start.8 = ((f32[16,12,128]{2,1,0:T(8,128)}), f32[16,12,128]{2,1,0:T(8,128)S(1)}, u32[]{:S(2)}, u32[]{:S(2)}) async-start(f32[16,12,128]{2,1,0:T(8,128)} %broadcast_in_dim.20), calls=%async_computation.10 | async-start | bytes 262144 | tf_op jit(solution)/shard_map/all_to_all | solution.py:58
  (38 other events, 363.4 us)
Sparse Core Ops, SparseCore 0:
  10.9 72.4 all-gather.3
  85.1 84.9 all-gather.5
  238.9 105.3 reduce-scatter.2
  346.6 52.0 reduce-scatter.4

commit v2 on v1

--- a/solution.py
+++ b/solution.py
@@ -77,33 +77,35 @@
     return sum(term.astype(WIDE) for term in [parts[0]] + came)
 
 
-def ring_gather(rows, beside=None):
+def ring_gather(rows):
     half = rows.shape[0] // 2
     first, second = rows[:half], rows[half:]
     before_first, after_second = ring(first, 1), ring(second, -1)
     before_second, after_first = ring(second, 1), ring(first, -1)
-    if beside is not None:
-        before_first, after_second, beside = tie(before_first, after_second, beside)
     across_first, across_second = ring(before_first, 1), ring(after_second, -1)
-    gathered = jnp.concatenate(
+    return jnp.concatenate(
         [
             first, second, before_first, before_second,
             after_first, after_second, across_first, across_second,
         ],
         0,
     )
-    return gathered if beside is None else (gathered, beside)
-
-
-def ring_sum_parts(rows):
+
+
+def ring_sum_parts(rows, later=None):
     own = rows.shape[0] // RING
     half = own // 2
     start, before, after, across = (rows[i * own : (i + 1) * own] for i in range(RING))
     from_before, from_after = ring(across[:half], 1), ring(across[half:], -1)
     second_after, first_before = ring(after[half:], 1), ring(before[:half], -1)
+    if later is not None:
+        from_before, from_after, second_after, first_before, later = tie(
+            from_before, from_after, second_after, first_before, later
+        )
     first_after = ring((after[:half].astype(WIDE) + from_before.astype(WIDE)).astype(LOW), 1)
     second_before = ring((before[half:].astype(WIDE) + from_after.astype(WIDE)).astype(LOW), -1)
-    return (start, first_after, second_after, first_before, second_before)
+    came = (start, first_after, second_after, first_before, second_before)
+    return came if later is None else (came, later)
 
 
 def ring_sum(rows):
@@ -152,14 +154,13 @@
     )(rows, weight, bias)
 
 
-def out_body(place_ref, heads_ref, weight_ref, out_ref):
+def out_body(heads_ref, weight_ref, out_ref):
     count, _, piece, _ = weight_ref.shape
     for block in range(count):
         value = dot_t(heads_ref[0], weight_ref[block, 0])
         for x in range(1, RING):
             value += dot_t(heads_ref[x], weight_ref[block, x])
-        here = slice(block * piece, (block + 1) * piece)
-        store_rows(out_ref.at[:, here], place_ref, value.astype(LOW))
+        out_ref[:, block * piece : (block + 1) * piece] = value.astype(LOW)
 
 
 def store_rows(out_ref, place_ref, value):
@@ -169,7 +170,7 @@
         out_ref[pl.ds(at, rows)] = value[slot * rows : (slot + 1) * rows]
 
 
-def out_project(places, heads, weight, at, blocks):
+def out_project(heads, weight, at, blocks):
     xs, count, cols = heads.shape
     zc, _, piece, _ = weight.shape
     return call(
@@ -178,14 +179,13 @@
         (zc // blocks,),
         [
             whole(heads.shape),
-            pl.BlockSpec((blocks, xs, piece, cols), lambda i, *_: (i, 0, 0, at)),
+            pl.BlockSpec((blocks, xs, piece, cols), lambda i: (i, 0, 0, at)),
         ],
-        pl.BlockSpec((count, blocks * piece), lambda i, *_: (0, i)),
+        pl.BlockSpec((count, blocks * piece), lambda i: (0, i)),
         2 * count * zc * piece * xs * cols,
         5 * 2**20,
-        prefetch=1,
         vmem=60,
-    )(places, heads, weight)
+    )(heads, weight)
 
 
 def heads_grad_body(rows_ref, weight_ref, out_ref):
@@ -270,7 +270,7 @@
     zc, xs, piece, cols = weight.shape
     size = cols // 2
     rows = whole((count, width))
-    vector = pl.BlockSpec((None, 1, size), lambda i, *_: (i, 0, 0))
+    vector = pl.BlockSpec((None, 1, size), lambda i, places: (places[RING + i], 0, 0))
     wide = pl.BlockSpec((count, size), lambda i, *_: (0, i))
     return call(
         ffn_first_body,
@@ -298,7 +298,7 @@
 
 
 def ffn_second_body(
-    place_ref, norm_ref, cot_ref, hidden_ref, grad_up_ref, down_ref, branch_ref, weight_grad_ref, total
+    norm_ref, cot_ref, hidden_ref, grad_up_ref, down_ref, branch_ref, weight_grad_ref, total
 ):
     width, cols = norm_ref.shape[1], down_ref.shape[-1]
     zc, piece, _ = weight_grad_ref.shape
@@ -314,24 +314,23 @@
         branch_ref[...] = total[...].astype(LOW)
 
 
-def ffn_second(places, norm_rows, cot_rows, hidden, grad_up, weight):
+def ffn_second(norm_rows, cot_rows, hidden, grad_up, weight):
     count, width = norm_rows.shape
     zc, xs, piece, cols = weight.shape
     size = cols // 2
     rows = whole((count, width))
-    wide = pl.BlockSpec((count, size), lambda i, *_: (0, i))
+    wide = pl.BlockSpec((count, size), lambda i: (0, i))
     return call(
         ffn_second_body,
         (struct((count, width), LOW), struct(weight.shape, LOW)),
         (xs,),
-        [rows, rows, wide, wide, pl.BlockSpec((zc, None, piece, size), lambda i, *_: (0, i, 0, 1))],
-        (rows, pl.BlockSpec((zc, None, piece, cols), lambda i, places: (0, places[i], 0, 0))),
+        [rows, rows, wide, wide, pl.BlockSpec((zc, None, piece, size), lambda i: (0, i, 0, 1))],
+        (rows, pl.BlockSpec((zc, None, piece, cols), lambda i: (0, i, 0, 0))),
         6 * count * width * xs * size,
         40 * 2**20,
         scratch=[pltpu.VMEM((count, width), WIDE)],
-        prefetch=1,
         vmem=56,
-    )(places, norm_rows, cot_rows, hidden, grad_up, weight)
+    )(norm_rows, cot_rows, hidden, grad_up, weight)
 
 
 def only_head(array, head):
@@ -615,10 +614,11 @@
     live_counts = jnp.concatenate(
         [jnp.sum(live_all.astype(jnp.int32), 1), y_at.astype(jnp.int32).reshape(1)]
     )
-    slots = jnp.arange(RING, dtype=jnp.int32)
-    apart = jnp.array([0, RING - 1, 1, 2], jnp.int32)
-    places = (y_at.astype(jnp.int32) + apart) % RING
-    x_places = (x_at.astype(jnp.int32) + apart) % RING
+    y_places, x_places = (
+        [((at + apart) % RING).astype(jnp.int32) for apart in (0, RING - 1, 1, 2)]
+        for at in (y_at, x_at)
+    )
+    places = jnp.stack(y_places + x_places)
     live_mine = lax.dynamic_slice_in_dim(live_all, head_at * own_rows, own_rows, 1)
     keep = live_mine.reshape(-1, 1).astype(WIDE)
 
@@ -631,10 +631,9 @@
     norm1 = ring_gather(norm_rows(inputs, ln1_gain, ln1_shift))
     flat_cot = cotangent.reshape(own, width)
     g_ffn = (keep * flat_cot.astype(WIDE)).astype(LOW)
-    norm1, g_ffn, w_ff = tie(norm1, g_ffn, w_ff)
-    cot_rows, w_ff = ring_gather(g_ffn, [ring(w_ff, step, "x") for step in (0, 1, -1, 2)])
+    norm1, w_ff = tie(norm1, [ring(w_ff, step, "x") for step in (0, 1, -1, 2)])
     w_ff = lax.all_gather(jnp.stack(w_ff), ROWS, axis=0)
-    norm1, cot_rows = tie(norm1, cot_rows)
+    norm1, cot_rows = tie(norm1, ring_gather(g_ffn))
 
     def mine(vector, cols):
         return lax.dynamic_index_in_dim(vector.reshape(RING, RING, cols), y_at, 1, False)
@@ -647,15 +646,15 @@
     qkv = swap(qkv, "x").reshape(rows5 + (3 * head_cols,))
     heads, exact, logs = attend(live_counts, qkv, head_cols)
     heads = swap(heads.reshape(RING, RING * own, head_cols), "x")
-    branch1 = ring_sum(out_project(slots, heads, w_attn, 3, 4)) + out_bias
+    branch1 = ring_sum(out_project(heads, w_attn, 3, 4)) + out_bias
     middle = inputs + keep * branch1
     norm2 = ring_gather(norm_rows(middle, ln2_gain, ln2_shift))
 
-    ff_bias = mine(up_bias, ff_cols)[x_places].reshape(RING, 1, ff_cols)
+    ff_bias = mine(up_bias, ff_cols).reshape(RING, 1, ff_cols)
     hidden, grad_up, g_norm2, up_bias_part = ffn_first(places, norm2, cot_rows, w_ff, ff_bias)
     g_norm2 = swap(g_norm2.reshape(RING, own, width), "y")
     g_norm2, branch2, ff_grad = tie(
-        g_norm2, *ffn_second(x_places, norm2, cot_rows, hidden, grad_up, w_ff)
+        g_norm2, *ffn_second(norm2, cot_rows, hidden, grad_up, w_ff)
     )
     ff_grad = settle(ff_grad)
     grad_mid, g_attn, sums2 = norm_back(g_norm2, middle, flat_cot, ln2_gain, keep)
@@ -669,11 +668,9 @@
     attn_grad = weight_grads(attn_rows, heads, 4 * head_cols, 3)
     d_qkv = swap(d_qkv.reshape(RING, RING * own, 3 * head_cols), "x")
 
-    up_bias_full = jnp.zeros((RING, RING, ff_cols), WIDE)
-    for slot in range(RING):
-        up_bias_full = lax.dynamic_update_slice(
-            up_bias_full, up_bias_part[slot][None], (x_places[slot], y_at, 0)
-        )
+    up_bias_full = lax.dynamic_update_slice_in_dim(
+        jnp.zeros((RING, RING, ff_cols), WIDE), up_bias_part.reshape(RING, 1, ff_cols), y_at, 1
+    )
     early = (
         sums2[2],
         sums2[0],
@@ -683,11 +680,10 @@
     )
     d_qkv, attn_grad, result = tie(d_qkv, attn_grad, result)
     attn_grad = weight_grads(norm1, d_qkv, 4 * head_cols, 0, attn_grad)
-    d_qkv, attn_grad, ff_grad = tie(d_qkv, attn_grad, ff_grad)
+    d_qkv, attn_grad = tie(d_qkv, attn_grad)
     attn_grad = settle(attn_grad)
-    g_norm1 = ring_sum_parts(out_project(slots, d_qkv, w_attn, 0, 2))
-    g_norm1, ff_grad = tie(g_norm1, swap(ff_grad, "x"))
-    ff_grad = jnp.sum(ff_grad.astype(WIDE), 0)
+    g_norm1, ff_grad = ring_sum_parts(out_project(d_qkv, w_attn, 0, 2), ff_grad)
+    ff_grad = ring_collect(ff_grad, "x")
     grad_tokens, sums1 = norm_back(g_norm1, tokens.reshape(own, width), grad_mid, ln1_gain)
     grad_tokens = grad_tokens.reshape(tokens.shape)
     d_sums = jnp.sum(d_sums, 0).reshape(3, head_cols)
@@ -697,7 +693,7 @@
         return lax.dynamic_update_slice_in_dim(blank, row[None], head_at, 0)
 
     part = collect_vectors(early + (sums1[0], sums1[1], placed(d_sums[0]), placed(d_sums[2])))
-    part, attn_grad = tie(part, attn_grad)
+    part, attn_grad, ff_grad = tie(part, attn_grad, ff_grad)
     here = [lax.dynamic_index_in_dim(attn_grad, x_places[i], 0, False) for i in range(RING)]
     attn_grad = ring_collect(here, "x")
     sizes = (width, width, width, RING * RING * ff_cols) + (width,) * 5

time: 451 us -> 418 us (0.927)
  waiting for transfers between devices: 138 us -> 120 us
  between operations: 23.2 us -> 15.7 us
  Pallas kernels: 113 us -> 108 us
    ppermute x45 -> x48, waiting for transfers between devices: 87.1 us -> 60.9 us  [ring(): lax.ppermute(array, axis, [(i, (i + step) % RING) for i in range(RING)])]
    ppermute x45 -> x48, starting transfers between devices: 51.7 us -> 64.7 us  [ring(): lax.ppermute(array, axis, [(i, (i + step) % RING) for i in range(RING)])]
    reduce_scatter x2, waiting for transfers between devices: 20.7 us -> 29.7 us  [settle(): return lax.psum_scatter(gradient, ROWS, scatter_dimension=0)]
    all_to_all x4 -> x3, starting transfers between devices: 20.6 us -> 13.7 us  [swap(): return lax.all_to_all(parts, axes, 0, 0)]
    unnamed x92 -> x70, local copies, waits for them, and re-layouts: 18.8 us -> 16 us
    all_to_all x4 -> x3, waiting for transfers between devices: 14.7 us -> 12.5 us  [swap(): return lax.all_to_all(parts, axes, 0, 0)]
  transfers between devices with their start and end apart: 56 -> 58, of which waited for: 30 -> 27; matrix products, arithmetic and copies ran while one was open for 12% -> 11% of each run, Pallas kernels for 21% -> 21%
where the time goes in v2:
time: 418 us; the launch traced here: 412 us
  waiting for transfers between devices  120 us (29%)
  Pallas kernels  108 us (26%)
  starting transfers between devices  93.3 us (22%)
  local copies, waits for them, and re-layouts  37.5 us (9%)
  blocking collectives  20.7 us (5%)
  other arithmetic  16.8 us (4%)
  between operations  15.7 us (4%)
    ppermute x48, starting transfers between devices, ring(): lax.ppermute(array, axis, [(i, (i + step) % RING) for i in range(RING)])  64.7 us
    ppermute x48, waiting for transfers between devices, ring(): lax.ppermute(array, axis, [(i, (i + step) % RING) for i in range(RING)])  60.9 us
    reduce_scatter x2, waiting for transfers between devices, settle(): return lax.psum_scatter(gradient, ROWS, scatter_dimension=0)  29.7 us
    pallas_call x1, Pallas kernels, ffn_first(): call(ffn_first_body, (struct((count, xs * size), LOW), struct((count, xs...  21.6 us
    pallas_call x1, Pallas kernels, ffn_second(): call(ffn_second_body, (struct((count, width), LOW), struct(weight.shape,...  21.5 us
    all_to_all x2, blocking collectives, swap(): return lax.all_to_all(parts, axes, 0, 0)  20.7 us
    unnamed x70, local copies, waits for them, and re-layouts  16 us
    pallas_call x2, Pallas kernels, weight_grads(): call(weight_grad_body, struct((8, xs, piece, total_cols), LOW), (xs,), [w...  14.3 us
  transfers between devices with their start and end apart: 58, of which 27 were waited for; matrix products, arithmetic and copies ran while one was open for 11% of the time, Pallas kernels for 21%

profile of v2, /device:TPU:1, one launch (start us, length us, event | category | flops | bytes accessed | tf_op | source)
XLA Modules:
  0.0 411.7 jit_solution(9112966027018140394)
XLA Ops:
  15.9 2.7 collective-permute-start.3
  24.1 3.2 collective-permute-done.1
  30.1 2.7 collective-permute-start.5
  32.8 4.6 %collective-permute-done.4 = bf16[64,2048]{1,0:T(8,128)(2,1)S(1)} collective-permute-done((bf16[64,2048]{1,0:T(8,128)(2,1)S(1)}, bf16[64,2048]{1,0:T(8,128)(2,1)S(1)}, u32[]{:S(2)}, u32[]{:S(2)}) %collective-permute-start.4) | collective-permute-done | bytes 262176 | tf_op jit(solution)/shard_map/ppermute | solution.py:72
  40.1 8.1 %collective-permute-done.8 = bf16[256,1024]{1,0:T(8,128)(2,1)S(1)} collective-permute-done((bf16[256,1024]{1,0:T(8,128)(2,1)S(1)}, bf16[256,1024]{1,0:T(8,128)(2,1)S(1)}, u32[]{:S(2)}, u32[]{:S(2)}) %collective-permute-start.8) | collective-permute-done | bytes 524320 | tf_op jit(solution)/shard_map/ppermute | solution.py:72
  52.0 2.7 collective-permute-start.11
  54.7 2.7 collective-permute-start.12
  60.8 3.5 collective-permute-start.14
  70.8 8.3 %shard_map.323 = bf16[4,512,384]{2,1,0:T(8,128)(2,1)} custom-call(bf16[512,2048]{1,0:T(8,128)(2,1)} %copy-done.8, bf16[8,4,256,512]{3,2,1,0:T(8,128)(2,1)} %bitcast.90, f32[4,1,384]{2,1,0:T(1,128)} %reshape.298.bias_ref), custom_call_target="tpu_custom_call" | custom-call | flops 3221225472 | bytes 10485760 | tf_op jit(solution)/shard_map/pallas_call | solution.py:141
  79.1 4.9 %all-to-all-start = ((bf16[4,512,384]{2,1,0:T(8,128)(2,1)}), bf16[4,512,384]{2,1,0:T(8,128)(2,1)}, u32[]{:S(2)}, u32[]{:S(2)}) async-start(bf16[4,512,384]{2,1,0:T(8,128)(2,1)} %shard_map.323), calls=%async_computation | async-start | bytes 3145728 | tf_op jit(solution)/shard_map/all_to_all | solution.py:66
  84.1 12.5 %all-to-all-done = bf16[4,512,384]{2,1,0:T(8,128)(2,1)} async-done(((bf16[4,512,384]{2,1,0:T(8,128)(2,1)}), bf16[4,512,384]{2,1,0:T(8,128)(2,1)}, u32[]{:S(2)}, u32[]{:S(2)}) %all-to-all-start) | async-done | bytes 1572896 | tf_op jit(solution)/shard_map/all_to_all | solution.py:66
  96.6 6.7 %shard_map.324 = (bf16[4,4,2,64,128]{4,3,2,1,0:T(8,128)(2,1)S(1)}, f32[2,1024,128]{2,1,0:T(8,128)S(1)}, f32[2,1024,128]{2,1,0:T(8,128)S(1)}) custom-call(s32[3]{0:T(128)S(1)} %pad_add_fusion.live_ref, bf16[4,4,2,64,384]{4,3,2,1,0:T(8,128)(2,1)} %bitcast.13.qkv_ref), custom_call_target="tpu_custom_call" | custom-call | flops 4000000000 | bytes 4194304 | tf_op jit(solution)/shard_map/pallas_call | solution.py:412
  104.3 10.1 %all_to_all.40.heads_ref.grad_ref = bf16[4,512,128]{2,1,0:T(8,128)(2,1)} all-to-all(bf16[4,512,128]{2,1,0:T(8,128)(2,1)S(1)} %bitcast.87), channel_id=1, replica_groups=mesh['z'=4,'c'=2,'x'=4,'y'=4] {'x'}, dimensions={0} | all-to-all | bytes 1048576 | tf_op jit(solution)/shard_map/all_to_all | solution.py:66
  114.4 4.9 %shard_map.325 = bf16[512,2048]{1,0:T(8,128)(2,1)} custom-call(bf16[4,512,128]{2,1,0:T(8,128)(2,1)} %all_to_all.40.heads_ref.grad_ref, bf16[8,4,256,512]{3,2,1,0:T(8,128)(2,1)} %bitcast.91), custom_call_target="tpu_custom_call" | custom-call | flops 1073741824 | bytes 5242880 | tf_op jit(solution)/shard_map/pallas_call | solution.py:176
  121.2 3.2 collective-permute-start.17
  125.8 2.7 collective-permute-done.15
  130.5 4.9 %collective-permute-done.16 = bf16[64,2048]{1,0:T(8,128)(2,1)S(1)} collective-permute-done((bf16[64,2048]{1,0:T(8,128)(2,1)S(1)}, bf16[64,2048]{1,0:T(8,128)(2,1)S(1)}, u32[]{:S(2)}, u32[]{:S(2)}) %collective-permute-start.16) | collective-permute-done | bytes 262176 | tf_op jit(solution)/shard_map/ppermute | solution.py:72
  136.0 3.3 collective-permute-done.18
  139.3 4.1 collective-permute-done.20
  146.1 2.8 collective-permute-start.24
  151.4 3.0 collective-permute-done.21
  155.2 2.8 collective-permute-start.26
  162.3 21.6 %shard_map.326 = (bf16[512,2048]{1,0:T(8,128)(2,1)}, bf16[512,2048]{1,0:T(8,128)(2,1)}, bf16[512,2048]{1,0:T(8,128)(2,1)}, f32[4,1,512]{2,1,0:T(1,128)}) custom-call(s32[8]{0:T(128)} %stack.50.place_ref, bf16[512,2048]{1,0:T(8,128)(2,1)} %constant_dynamic-update-slice_fusion.14.norm_ref, bf16[512,2048]{1,0:T(8,128)(2,1)} %constant_dynamic-update-slice_fusion.7.cot_ref, ...), custom_call_target="tpu_custom_call" | custom-call | flops 12884901888 | bytes 26214400 | tf_op jit(solution)/shard_map/pallas_call | solution.py:275
  183.9 4.5 %all-to-all-start.2 = ((bf16[4,128,2048]{2,1,0:T(8,128)(2,1)}), bf16[4,128,2048]{2,1,0:T(8,128)(2,1)}, u32[]{:S(2)}, u32[]{:S(2)}) async-start(bf16[4,128,2048]{2,1,0:T(8,128)(2,1)} %bitcast.98), calls=%async_computation.2 | async-start | bytes 4194304 | tf_op jit(solution)/shard_map/all_to_all | solution.py:66
  188.4 21.5 %shard_map.327 = (bf16[512,2048]{1,0:T(8,128)(2,1)}, bf16[8,4,256,1024]{3,2,1,0:T(8,128)(2,1)}) custom-call(bf16[512,2048]{1,0:T(8,128)(2,1)} %constant_dynamic-update-slice_fusion.14.norm_ref, bf16[512,2048]{1,0:T(8,128)(2,1)} %constant_dynamic-update-slice_fusion.7.cot_ref, bf16[512,2048]{1,0:T(8,128)(2,1)} %get-tuple-element.69.hidden_ref, ...), custom_call_target="tpu_custom_call" | custom-call | flops 12884901888 | bytes 41943040 | tf_op jit(solution)/shard_map/pallas_call | solution.py:323
  210.1 3.5 shard_map.328
  218.9 3.7 collective-permute-done.27
  223.4 2.7 collective-permute-start.32
  230.5 5.8 %shard_map.329 = bf16[4,512,128]{2,1,0:T(8,128)(2,1)} custom-call(bf16[512,2048]{1,0:T(8,128)(2,1)} %constant_dynamic-update-slice_fusion.21.rows_ref, bf16[8,4,256,512]{3,2,1,0:T(8,128)(2,1)} %bitcast.92), custom_call_target="tpu_custom_call" | custom-call | flops 1073741824 | bytes 5242880 | tf_op jit(solution)/shard_map/pallas_call | solution.py:199
  236.3 10.6 %all_to_all.41 = bf16[4,512,128]{2,1,0:T(8,128)(2,1)S(1)} all-to-all(bf16[4,512,128]{2,1,0:T(8,128)(2,1)} %shard_map.329), channel_id=1, replica_groups=mesh['z'=4,'c'=2,'x'=4,'y'=4] {'x'}, dimensions={0} | all-to-all | bytes 1048576 | tf_op jit(solution)/shard_map/all_to_all | solution.py:66
  249.4 10.6 %shard_map.330 = (bf16[4,4,2,64,384]{4,3,2,1,0:T(8,128)(2,1)}, f32[2,1,384]{2,1,0:T(1,128)S(1)}) custom-call(s32[3]{0:T(128)S(1)} %pad_add_fusion.live_ref, bf16[4,4,2,64,384]{4,3,2,1,0:T(8,128)(2,1)} %bitcast.13.qkv_ref, bf16[4,4,2,64,128]{4,3,2,1,0:T(8,128)(2,1)S(1)} %bitcast.86, f32[2,1024,128]{2,1,0:T(8,128)S(1)} %copy-done.5, f32[2,1024,128]{2,1,0:T(8,128)S(1)} %copy-done.7), custom_call_target="tpu_custom_call" | custom-call | flops 8000000000 | bytes 8388608 | tf_op jit(solution)/shard_map/pallas_call | solution.py:489
  260.0 4.4 %all-to-all-start.4 = ((bf16[4,512,384]{2,1,0:T(8,128)(2,1)}), bf16[4,512,384]{2,1,0:T(8,128)(2,1)}, u32[]{:S(2)}, u32[]{:S(2)}) async-start(bf16[4,512,384]{2,1,0:T(8,128)(2,1)} %bitcast.32), calls=%async_computation.4 | async-start | bytes 3145728 | tf_op jit(solution)/shard_map/all_to_all | solution.py:66
  266.9 2.7 collective-permute-start.33
  270.8 6.1 %shard_map.331.refs_0_ = bf16[8,4,256,512]{3,2,1,0:T(8,128)(2,1)} custom-call(bf16[512,2048]{1,0:T(8,128)(2,1)} %constant_dynamic-update-slice_fusion.21.rows_ref, bf16[4,512,128]{2,1,0:T(8,128)(2,1)} %all_to_all.40.heads_ref.grad_ref), custom_call_target="tpu_custom_call" | custom-call | flops 1073741824 | bytes 15728640 | tf_op jit(solution)/shard_map/pallas_call | solution.py:224
  277.0 4.7 %collective-permute-done.33 = bf16[128,2048]{1,0:T(8,128)(2,1)S(1)} collective-permute-done((bf16[128,2048]{1,0:T(8,128)(2,1)}, bf16[128,2048]{1,0:T(8,128)(2,1)S(1)}, u32[]{:S(2)}, u32[]{:S(2)}) %collective-permute-start.33) | collective-permute-done | bytes 524320 | tf_op jit(solution)/shard_map/ppermute | solution.py:72
  281.7 3.4 collective-permute-done.34
  287.6 8.2 %shard_map.332 = bf16[8,4,256,512]{3,2,1,0:T(8,128)(2,1)} custom-call(bf16[512,2048]{1,0:T(8,128)(2,1)} %copy-done.8, bf16[4,512,384]{2,1,0:T(8,128)(2,1)} %all-to-all-done.4.grad_ref.heads_ref, bf16[8,4,256,512]{3,2,1,0:T(8,128)(2,1)} %shard_map.331.refs_0_), custom_call_target="tpu_custom_call", output_to_operand_aliasing={{}: (2, {})} | custom-call | flops 3221225472 | bytes 15728640 | tf_op jit(solution)/shard_map/pallas_call | solution.py:224
  296.7 8.4 %shard_map.333 = bf16[512,2048]{1,0:T(8,128)(2,1)} custom-call(bf16[4,512,384]{2,1,0:T(8,128)(2,1)} %all-to-all-done.4.grad_ref.heads_ref, bf16[8,4,256,512]{3,2,1,0:T(8,128)(2,1)} %bitcast.93), custom_call_target="tpu_custom_call" | custom-call | flops 3221225472 | bytes 5242880 | tf_op jit(solution)/shard_map/pallas_call | solution.py:176
  307.2 2.7 collective-permute-start.37
  309.8 2.9 collective-permute-start.39
  314.2 2.8 collective-permute-done.38.refs_2_
  317.0 3.3 reduce-scatter.3.cloned.1.call-done
  334.2 4.1 all-to-all-start.5
  338.4 7.9 %all-to-all-done.5 = f32[16,12,128]{2,1,0:T(8,128)S(1)} async-done(((f32[16,12,128]{2,1,0:T(8,128)}), f32[16,12,128]{2,1,0:T(8,128)S(1)}, u32[]{:S(2)}, u32[]{:S(2)}) %all-to-all-start.5) | async-done | bytes 98336 | tf_op jit(solution)/shard_map/all_to_all | solution.py:62
  348.2 26.4 %reduce-scatter.5.cloned.1.call-done = bf16[1,4,256,512]{3,2,1,0:T(8,128)(2,1)} async-done(((bf16[8,4,256,512]{3,2,1,0:T(8,128)(2,1)}), bf16[1,4,256,512]{3,2,1,0:T(8,128)(2,1)}) %reduce-scatter.5.cloned.1.call-update) | async-done | bytes 1048592 | tf_op jit(solution)/shard_map/reduce_scatter | solution.py:129
  375.3 4.7 %all-to-all-start.6 = ((f32[8,12,128]{2,1,0:T(8,128)}), f32[8,12,128]{2,1,0:T(8,128)S(1)}, u32[]{:S(2)}, u32[]{:S(2)}) async-start(f32[8,12,128]{2,1,0:T(8,128)} %broadcast_in_dim.16), calls=%async_computation.8 | async-start | bytes 131072 | tf_op jit(solution)/shard_map/all_to_all | solution.py:58
  386.0 6.0 %all-to-all-start.7 = ((f32[16,12,128]{2,1,0:T(8,128)}), f32[16,12,128]{2,1,0:T(8,128)S(1)}, u32[]{:S(2)}, u32[]{:S(2)}) async-start(f32[16,12,128]{2,1,0:T(8,128)} %broadcast_in_dim.17), calls=%async_computation.9 | async-start | bytes 262144 | tf_op jit(solution)/shard_map/all_to_all | solution.py:58
  393.1 8.5 %all-to-all-done.7 = f32[16,12,128]{2,1,0:T(8,128)S(1)} async-done(((f32[16,12,128]{2,1,0:T(8,128)}), f32[16,12,128]{2,1,0:T(8,128)S(1)}, u32[]{:S(2)}, u32[]{:S(2)}) %all-to-all-start.7) | async-done | bytes 98336 | tf_op jit(solution)/shard_map/all_to_all | solution.py:58
  (235 shorter events, 100.1 us)
Async XLA Ops:
  7.2 63.6 %all-gather.4.cloned.1.call-start = ((), (), s32[]{:S(2)}) async-start(), calls=%async_computation.10 | async-start | bytes 8650752 | tf_op jit(solution)/shard_map/all_gather | solution.py:124
  10.1 152.3 %all-gather.6.cloned.1.call-start = ((), (), s32[]{:S(2)}) async-start(), calls=%async_computation.13 | async-start | bytes 18874368 | tf_op jit(solution)/shard_map/all_gather | solution.py:635
  12.2 9.5 %collective-permute-start = (bf16[64,2048]{1,0:T(8,128)(2,1)S(1)}, bf16[64,2048]{1,0:T(8,128)(2,1)S(1)}, u32[]{:S(2)}, u32[]{:S(2)}) collective-permute-start(bf16[64,2048]{1,0:T(8,128)(2,1)S(1)} %get-tuple-element.145), channel_id=1, source_target_pairs={{0,1},{1,2},{2,3},{3,0},{4,5},{5,6},{6,7},{7,4},{8,9},{9,10},{10,1... | collective-permute-start | bytes 786440 | tf_op jit(solution)/shard_map/ppermute | solution.py:72
  14.4 15.6 %collective-permute-start.2 = (bf16[64,2048]{1,0:T(8,128)(2,1)S(1)}, bf16[64,2048]{1,0:T(8,128)(2,1)S(1)}, u32[]{:S(2)}, u32[]{:S(2)}) collective-permute-start(bf16[64,2048]{1,0:T(8,128)(2,1)S(1)} %get-tuple-element.145), channel_id=1, source_target_pairs={{0,3},{1,0},{2,1},{3,2},{4,7},{5,4},{6,5},{7,6},{8,11},{9,8},{10,9... | collective-permute-start | bytes 786440 | tf_op jit(solution)/shard_map/ppermute | solution.py:72
  15.9 11.4 %collective-permute-start.1 = (bf16[64,2048]{1,0:T(8,128)(2,1)S(1)}, bf16[64,2048]{1,0:T(8,128)(2,1)S(1)}, u32[]{:S(2)}, u32[]{:S(2)}) collective-permute-start(bf16[64,2048]{1,0:T(8,128)(2,1)S(1)} %get-tuple-element.144), channel_id=1, source_target_pairs={{0,1},{1,2},{2,3},{3,0},{4,5},{5,6},{6,7},{7,4},{8,9},{9,10},{10,1... | collective-permute-start | bytes 786440 | tf_op jit(solution)/shard_map/ppermute | solution.py:72
  15.9 14.2 %collective-permute-start.3 = (bf16[64,2048]{1,0:T(8,128)(2,1)S(1)}, bf16[64,2048]{1,0:T(8,128)(2,1)S(1)}, u32[]{:S(2)}, u32[]{:S(2)}) collective-permute-start(bf16[64,2048]{1,0:T(8,128)(2,1)S(1)} %get-tuple-element.144), channel_id=1, source_target_pairs={{0,3},{1,0},{2,1},{3,2},{4,7},{5,4},{6,5},{7,6},{8,11},{9,8},{10,9... | collective-permute-start | bytes 786440 | tf_op jit(solution)/shard_map/ppermute | solution.py:72
  18.7 18.8 %collective-permute-start.6 = (bf16[256,1024]{1,0:T(8,128)(2,1)S(1)}, bf16[256,1024]{1,0:T(8,128)(2,1)S(1)}, u32[]{:S(2)}, u32[]{:S(2)}) collective-permute-start(bf16[256,1024]{1,0:T(8,128)(2,1)S(1)} %pad_maximum_fusion.2), channel_id=1, source_target_pairs={{0,4},{4,8},{8,12},{12,0},{1,5},{5,9},{9,13},{13,1},{2,6},{6,10},{... | collective-permute-start | bytes 1572872 | tf_op jit(solution)/shard_map/ppermute | solution.py:72
  21.7 18.4 %collective-permute-start.7 = (bf16[256,1024]{1,0:T(8,128)(2,1)S(1)}, bf16[256,1024]{1,0:T(8,128)(2,1)S(1)}, u32[]{:S(2)}, u32[]{:S(2)}) collective-permute-start(bf16[256,1024]{1,0:T(8,128)(2,1)S(1)} %pad_maximum_fusion.2), channel_id=1, source_target_pairs={{0,12},{4,0},{8,4},{12,8},{1,13},{5,1},{9,5},{13,9},{2,14},{6,2},{... | collective-permute-start | bytes 1572872 | tf_op jit(solution)/shard_map/ppermute | solution.py:72
  27.3 20.9 %collective-permute-start.8 = (bf16[256,1024]{1,0:T(8,128)(2,1)S(1)}, bf16[256,1024]{1,0:T(8,128)(2,1)S(1)}, u32[]{:S(2)}, u32[]{:S(2)}) collective-permute-start(bf16[256,1024]{1,0:T(8,128)(2,1)S(1)} %pad_maximum_fusion.2), channel_id=1, source_target_pairs={{0,8},{4,12},{8,0},{12,4},{1,9},{5,13},{9,1},{13,5},{2,10},{6,14},... | collective-permute-start | bytes 1572872 | tf_op jit(solution)/shard_map/ppermute | solution.py:72
  30.0 7.4 %collective-permute-start.4 = (bf16[64,2048]{1,0:T(8,128)(2,1)S(1)}, bf16[64,2048]{1,0:T(8,128)(2,1)S(1)}, u32[]{:S(2)}, u32[]{:S(2)}) collective-permute-start(bf16[64,2048]{1,0:T(8,128)(2,1)S(1)} %collective-permute-done), channel_id=1, source_target_pairs={{0,1},{1,2},{2,3},{3,0},{4,5},{5,6},{6,7},{7,4},{8,9},{9,10},{10,1... | collective-permute-start | bytes 786440 | tf_op jit(solution)/shard_map/ppermute | solution.py:72
  30.1 7.4 %collective-permute-start.5 = (bf16[64,2048]{1,0:T(8,128)(2,1)S(1)}, bf16[64,2048]{1,0:T(8,128)(2,1)S(1)}, u32[]{:S(2)}, u32[]{:S(2)}) collective-permute-start(bf16[64,2048]{1,0:T(8,128)(2,1)S(1)} %collective-permute-done.3), channel_id=1, source_target_pairs={{0,3},{1,0},{2,1},{3,2},{4,7},{5,4},{6,5},{7,6},{8,11},{9,8},{10,9... | collective-permute-start | bytes 786440 | tf_op jit(solution)/shard_map/ppermute | solution.py:72
  52.0 13.0 %collective-permute-start.11 = (bf16[64,2048]{1,0:T(8,128)(2,1)S(1)}, bf16[64,2048]{1,0:T(8,128)(2,1)S(1)}, u32[]{:S(2)}, u32[]{:S(2)}) collective-permute-start(bf16[64,2048]{1,0:T(8,128)(2,1)S(1)} %get-tuple-element.143), channel_id=1, source_target_pairs={{0,3},{1,0},{2,1},{3,2},{4,7},{5,4},{6,5},{7,6},{8,11},{9,8},{10,9... | collective-permute-start | bytes 786440 | tf_op jit(solution)/shard_map/ppermute | solution.py:72
  54.7 9.6 %collective-permute-start.10 = (bf16[64,2048]{1,0:T(8,128)(2,1)S(1)}, bf16[64,2048]{1,0:T(8,128)(2,1)S(1)}, u32[]{:S(2)}, u32[]{:S(2)}) collective-permute-start(bf16[64,2048]{1,0:T(8,128)(2,1)S(1)} %get-tuple-element.142), channel_id=1, source_target_pairs={{0,1},{1,2},{2,3},{3,0},{4,5},{5,6},{6,7},{7,4},{8,9},{9,10},{10,1... | collective-permute-start | bytes 786440 | tf_op jit(solution)/shard_map/ppermute | solution.py:72
  58.8 9.5 %collective-permute-start.13 = (bf16[64,2048]{1,0:T(8,128)(2,1)S(1)}, bf16[64,2048]{1,0:T(8,128)(2,1)S(1)}, u32[]{:S(2)}, u32[]{:S(2)}) collective-permute-start(bf16[64,2048]{1,0:T(8,128)(2,1)S(1)} %collective-permute-done.9), channel_id=1, source_target_pairs={{0,1},{1,2},{2,3},{3,0},{4,5},{5,6},{6,7},{7,4},{8,9},{9,10},{10,1... | collective-permute-start | bytes 786440 | tf_op jit(solution)/shard_map/ppermute | solution.py:72
  60.8 9.3 %collective-permute-start.14 = (bf16[64,2048]{1,0:T(8,128)(2,1)S(1)}, bf16[64,2048]{1,0:T(8,128)(2,1)S(1)}, u32[]{:S(2)}, u32[]{:S(2)}) collective-permute-start(bf16[64,2048]{1,0:T(8,128)(2,1)S(1)} %collective-permute-done.12), channel_id=1, source_target_pairs={{0,3},{1,0},{2,1},{3,2},{4,7},{5,4},{6,5},{7,6},{8,11},{9,8},{10,9... | collective-permute-start | bytes 786440 | tf_op jit(solution)/shard_map/ppermute | solution.py:72
  79.1 17.5 %all-to-all-start = ((bf16[4,512,384]{2,1,0:T(8,128)(2,1)}), bf16[4,512,384]{2,1,0:T(8,128)(2,1)}, u32[]{:S(2)}, u32[]{:S(2)}) async-start(bf16[4,512,384]{2,1,0:T(8,128)(2,1)} %shard_map.323), calls=%async_computation | async-start | bytes 3145728 | tf_op jit(solution)/shard_map/all_to_all | solution.py:66
  120.8 7.7 %collective-permute-start.15 = (bf16[64,2048]{1,0:T(8,128)(2,1)S(1)}, bf16[64,2048]{1,0:T(8,128)(2,1)S(1)}, u32[]{:S(2)}, u32[]{:S(2)}) collective-permute-start(bf16[64,2048]{1,0:T(8,128)(2,1)S(1)} %get-tuple-element.123), channel_id=1, source_target_pairs={{0,1},{1,2},{2,3},{3,0},{4,5},{5,6},{6,7},{7,4},{8,9},{9,10},{10,1... | collective-permute-start | bytes 786440 | tf_op jit(solution)/shard_map/ppermute | solution.py:72
  121.2 7.5 %collective-permute-start.17 = (bf16[64,2048]{1,0:T(8,128)(2,1)S(1)}, bf16[64,2048]{1,0:T(8,128)(2,1)S(1)}, u32[]{:S(2)}, u32[]{:S(2)}) collective-permute-start(bf16[64,2048]{1,0:T(8,128)(2,1)S(1)} %get-tuple-element.126), channel_id=1, source_target_pairs={{0,3},{1,0},{2,1},{3,2},{4,7},{5,4},{6,5},{7,6},{8,11},{9,8},{10,9... | collective-permute-start | bytes 786440 | tf_op jit(solution)/shard_map/ppermute | solution.py:72
  128.7 10.6 %collective-permute-start.18 = (bf16[64,2048]{1,0:T(8,128)(2,1)S(1)}, bf16[64,2048]{1,0:T(8,128)(2,1)S(1)}, u32[]{:S(2)}, u32[]{:S(2)}) collective-permute-start(bf16[64,2048]{1,0:T(8,128)(2,1)S(1)} %get-tuple-element.125), channel_id=1, source_target_pairs={{0,1},{1,2},{2,3},{3,0},{4,5},{5,6},{6,7},{7,4},{8,9},{9,10},{10,1... | collective-permute-start | bytes 786440 | tf_op jit(solution)/shard_map/ppermute | solution.py:72
  135.6 7.7 %collective-permute-start.20 = (bf16[64,2048]{1,0:T(8,128)(2,1)S(1)}, bf16[64,2048]{1,0:T(8,128)(2,1)S(1)}, u32[]{:S(2)}, u32[]{:S(2)}) collective-permute-start(bf16[64,2048]{1,0:T(8,128)(2,1)S(1)} %get-tuple-element.122), channel_id=1, source_target_pairs={{0,3},{1,0},{2,1},{3,2},{4,7},{5,4},{6,5},{7,6},{8,11},{9,8},{10,9... | collective-permute-start | bytes 786440 | tf_op jit(solution)/shard_map/ppermute | solution.py:72
  145.9 8.5 %collective-permute-start.21 = (bf16[64,2048]{1,0:T(8,128)(2,1)S(1)}, bf16[64,2048]{1,0:T(8,128)(2,1)S(1)}, u32[]{:S(2)}, u32[]{:S(2)}) collective-permute-start(bf16[64,2048]{1,0:T(8,128)(2,1)S(1)} %get-tuple-element.141), channel_id=1, source_target_pairs={{0,1},{1,2},{2,3},{3,0},{4,5},{5,6},{6,7},{7,4},{8,9},{9,10},{10,1... | collective-permute-start | bytes 786440 | tf_op jit(solution)/shard_map/ppermute | solution.py:72
  146.0 12.0 %collective-permute-start.22 = (bf16[64,2048]{1,0:T(8,128)(2,1)S(1)}, bf16[64,2048]{1,0:T(8,128)(2,1)S(1)}, u32[]{:S(2)}, u32[]{:S(2)}) collective-permute-start(bf16[64,2048]{1,0:T(8,128)(2,1)S(1)} %get-tuple-element.140), channel_id=1, source_target_pairs={{0,1},{1,2},{2,3},{3,0},{4,5},{5,6},{6,7},{7,4},{8,9},{9,10},{10,1... | collective-permute-start | bytes 786440 | tf_op jit(solution)/shard_map/ppermute | solution.py:72
  146.1 9.1 %collective-permute-start.24 = (bf16[64,2048]{1,0:T(8,128)(2,1)S(1)}, bf16[64,2048]{1,0:T(8,128)(2,1)S(1)}, u32[]{:S(2)}, u32[]{:S(2)}) collective-permute-start(bf16[64,2048]{1,0:T(8,128)(2,1)S(1)} %get-tuple-element.140), channel_id=1, source_target_pairs={{0,3},{1,0},{2,1},{3,2},{4,7},{5,4},{6,5},{7,6},{8,11},{9,8},{10,9... | collective-permute-start | bytes 786440 | tf_op jit(solution)/shard_map/ppermute | solution.py:72
  150.1 8.7 %collective-permute-start.23 = (bf16[64,2048]{1,0:T(8,128)(2,1)S(1)}, bf16[64,2048]{1,0:T(8,128)(2,1)S(1)}, u32[]{:S(2)}, u32[]{:S(2)}) collective-permute-start(bf16[64,2048]{1,0:T(8,128)(2,1)S(1)} %get-tuple-element.141), channel_id=1, source_target_pairs={{0,3},{1,0},{2,1},{3,2},{4,7},{5,4},{6,5},{7,6},{8,11},{9,8},{10,9... | collective-permute-start | bytes 786440 | tf_op jit(solution)/shard_map/ppermute | solution.py:72
  183.9 26.0 %all-to-all-start.2 = ((bf16[4,128,2048]{2,1,0:T(8,128)(2,1)}), bf16[4,128,2048]{2,1,0:T(8,128)(2,1)}, u32[]{:S(2)}, u32[]{:S(2)}) async-start(bf16[4,128,2048]{2,1,0:T(8,128)(2,1)} %bitcast.98), calls=%async_computation.2 | async-start | bytes 4194304 | tf_op jit(solution)/shard_map/all_to_all | solution.py:66
  188.4 131.9 %reduce-scatter.3.cloned.1.call-start = ((), (), s32[]{:S(2)}) async-start(), calls=%async_computation.11 | async-start | bytes 18874368 | tf_op jit(solution)/shard_map/reduce_scatter | solution.py:129
  213.6 9.0 %collective-permute-start.27 = (bf16[64,2048]{1,0:T(8,128)(2,1)S(1)}, bf16[64,2048]{1,0:T(8,128)(2,1)S(1)}, u32[]{:S(2)}, u32[]{:S(2)}) collective-permute-start(bf16[64,2048]{1,0:T(8,128)(2,1)S(1)} %get-tuple-element.139), channel_id=1, source_target_pairs={{0,1},{1,2},{2,3},{3,0},{4,5},{5,6},{6,7},{7,4},{8,9},{9,10},{10,1... | collective-permute-start | bytes 786440 | tf_op jit(solution)/shard_map/ppermute | solution.py:72
  215.1 11.0 %collective-permute-start.28 = (bf16[64,2048]{1,0:T(8,128)(2,1)S(1)}, bf16[64,2048]{1,0:T(8,128)(2,1)S(1)}, u32[]{:S(2)}, u32[]{:S(2)}) collective-permute-start(bf16[64,2048]{1,0:T(8,128)(2,1)S(1)} %get-tuple-element.138), channel_id=1, source_target_pairs={{0,1},{1,2},{2,3},{3,0},{4,5},{5,6},{6,7},{7,4},{8,9},{9,10},{10,1... | collective-permute-start | bytes 786440 | tf_op jit(solution)/shard_map/ppermute | solution.py:72
  216.2 7.1 %collective-permute-start.30 = (bf16[64,2048]{1,0:T(8,128)(2,1)S(1)}, bf16[64,2048]{1,0:T(8,128)(2,1)S(1)}, u32[]{:S(2)}, u32[]{:S(2)}) collective-permute-start(bf16[64,2048]{1,0:T(8,128)(2,1)S(1)} %get-tuple-element.138), channel_id=1, source_target_pairs={{0,3},{1,0},{2,1},{3,2},{4,7},{5,4},{6,5},{7,6},{8,11},{9,8},{10,9... | collective-permute-start | bytes 786440 | tf_op jit(solution)/shard_map/ppermute | solution.py:72
  218.6 8.2 %collective-permute-start.29 = (bf16[64,2048]{1,0:T(8,128)(2,1)S(1)}, bf16[64,2048]{1,0:T(8,128)(2,1)S(1)}, u32[]{:S(2)}, u32[]{:S(2)}) collective-permute-start(bf16[64,2048]{1,0:T(8,128)(2,1)S(1)} %get-tuple-element.139), channel_id=1, source_target_pairs={{0,3},{1,0},{2,1},{3,2},{4,7},{5,4},{6,5},{7,6},{8,11},{9,8},{10,9... | collective-permute-start | bytes 786440 | tf_op jit(solution)/shard_map/ppermute | solution.py:72
  260.0 27.7 %all-to-all-start.4 = ((bf16[4,512,384]{2,1,0:T(8,128)(2,1)}), bf16[4,512,384]{2,1,0:T(8,128)(2,1)}, u32[]{:S(2)}, u32[]{:S(2)}) async-start(bf16[4,512,384]{2,1,0:T(8,128)(2,1)} %bitcast.32), calls=%async_computation.4 | async-start | bytes 3145728 | tf_op jit(solution)/shard_map/all_to_all | solution.py:66
  264.3 110.3 %reduce-scatter.5.cloned.1.call-start = ((), (), s32[]{:S(2)}) async-start(), calls=%async_computation.12 | async-start | bytes 9437184 | tf_op jit(solution)/shard_map/reduce_scatter | solution.py:129
  266.9 14.8 %collective-permute-start.33 = (bf16[128,2048]{1,0:T(8,128)(2,1)}, bf16[128,2048]{1,0:T(8,128)(2,1)S(1)}, u32[]{:S(2)}, u32[]{:S(2)}) collective-permute-start(bf16[128,2048]{1,0:T(8,128)(2,1)} %get-tuple-element.118), channel_id=1, source_target_pairs={{0,3},{1,0},{2,1},{3,2},{4,7},{5,4},{6,5},{7,6},{8,11},{9,8},{10,9... | collective-permute-start | bytes 1572872 | tf_op jit(solution)/shard_map/ppermute | solution.py:72
  269.6 15.5 %collective-permute-start.34 = (bf16[128,2048]{1,0:T(8,128)(2,1)}, bf16[128,2048]{1,0:T(8,128)(2,1)S(1)}, u32[]{:S(2)}, u32[]{:S(2)}) collective-permute-start(bf16[128,2048]{1,0:T(8,128)(2,1)} %get-tuple-element.120), channel_id=1, source_target_pairs={{0,1},{1,2},{2,3},{3,0},{4,5},{5,6},{6,7},{7,4},{8,9},{9,10},{10,1... | collective-permute-start | bytes 1572872 | tf_op jit(solution)/shard_map/ppermute | solution.py:72
  269.6 15.5 %collective-permute-start.35 = (bf16[128,2048]{1,0:T(8,128)(2,1)}, bf16[128,2048]{1,0:T(8,128)(2,1)}, u32[]{:S(2)}, u32[]{:S(2)}) collective-permute-start(bf16[128,2048]{1,0:T(8,128)(2,1)} %get-tuple-element.119), channel_id=1, source_target_pairs={{0,2},{1,3},{2,0},{3,1},{4,6},{5,7},{6,4},{7,5},{8,10},{9,11},{10,... | collective-permute-start | bytes 1572872 | tf_op jit(solution)/shard_map/ppermute | solution.py:72
  309.8 7.2 %collective-permute-start.38 = (bf16[64,2048]{1,0:T(8,128)(2,1)}, bf16[64,2048]{1,0:T(8,128)(2,1)S(1)}, u32[]{:S(2)}, u32[]{:S(2)}) collective-permute-start(bf16[64,2048]{1,0:T(8,128)(2,1)} %get-tuple-element.115), channel_id=1, source_target_pairs={{0,1},{1,2},{2,3},{3,0},{4,5},{5,6},{6,7},{7,4},{8,9},{9,10},{10,1... | collective-permute-start | bytes 786440 | tf_op jit(solution)/shard_map/ppermute | solution.py:72
  309.8 7.2 %collective-permute-start.39 = (bf16[64,2048]{1,0:T(8,128)(2,1)S(1)}, bf16[64,2048]{1,0:T(8,128)(2,1)S(1)}, u32[]{:S(2)}, u32[]{:S(2)}) collective-permute-start(bf16[64,2048]{1,0:T(8,128)(2,1)S(1)} %get-tuple-element.114), channel_id=1, source_target_pairs={{0,3},{1,0},{2,1},{3,2},{4,7},{5,4},{6,5},{7,6},{8,11},{9,8},{10,9... | collective-permute-start | bytes 786440 | tf_op jit(solution)/shard_map/ppermute | solution.py:72
  321.5 9.5 %collective-permute-start.40 = (bf16[64,2048]{1,0:T(8,128)(2,1)S(1)}, bf16[64,2048]{1,0:T(8,128)(2,1)S(1)}, u32[]{:S(2)}, u32[]{:S(2)}) collective-permute-start(bf16[64,2048]{1,0:T(8,128)(2,1)S(1)} %get-tuple-element.113), channel_id=1, source_target_pairs={{0,1},{1,2},{2,3},{3,0},{4,5},{5,6},{6,7},{7,4},{8,9},{9,10},{10,1... | collective-permute-start | bytes 786440 | tf_op jit(solution)/shard_map/ppermute | solution.py:72
  322.8 8.2 %collective-permute-start.41 = (bf16[64,2048]{1,0:T(8,128)(2,1)S(1)}, bf16[64,2048]{1,0:T(8,128)(2,1)S(1)}, u32[]{:S(2)}, u32[]{:S(2)}) collective-permute-start(bf16[64,2048]{1,0:T(8,128)(2,1)S(1)} %get-tuple-element.112), channel_id=1, source_target_pairs={{0,3},{1,0},{2,1},{3,2},{4,7},{5,4},{6,5},{7,6},{8,11},{9,8},{10,9... | collective-permute-start | bytes 786440 | tf_op jit(solution)/shard_map/ppermute | solution.py:72
  326.8 19.5 %collective-permute-start.42 = (bf16[256,1024]{1,0:T(8,128)(2,1)}, bf16[256,1024]{1,0:T(8,128)(2,1)}, u32[]{:S(2)}, u32[]{:S(2)}) collective-permute-start(bf16[256,1024]{1,0:T(8,128)(2,1)} %get-tuple-element.109), channel_id=1, source_target_pairs={{0,12},{4,0},{8,4},{12,8},{1,13},{5,1},{9,5},{13,9},{2,14},{6,2},{... | collective-permute-start | bytes 1572872 | tf_op jit(solution)/shard_map/ppermute | solution.py:72
  329.2 17.1 %collective-permute-start.43 = (bf16[256,1024]{1,0:T(8,128)(2,1)}, bf16[256,1024]{1,0:T(8,128)(2,1)}, u32[]{:S(2)}, u32[]{:S(2)}) collective-permute-start(bf16[256,1024]{1,0:T(8,128)(2,1)} %get-tuple-element.111), channel_id=1, source_target_pairs={{0,4},{4,8},{8,12},{12,0},{1,5},{5,9},{9,13},{13,1},{2,6},{6,10},{... | collective-permute-start | bytes 1572872 | tf_op jit(solution)/shard_map/ppermute | solution.py:72
  329.2 17.2 %collective-permute-start.44 = (bf16[256,1024]{1,0:T(8,128)(2,1)}, bf16[256,1024]{1,0:T(8,128)(2,1)}, u32[]{:S(2)}, u32[]{:S(2)}) collective-permute-start(bf16[256,1024]{1,0:T(8,128)(2,1)} %get-tuple-element.110), channel_id=1, source_target_pairs={{0,8},{4,12},{8,0},{12,4},{1,9},{5,13},{9,1},{13,5},{2,10},{6,14},... | collective-permute-start | bytes 1572872 | tf_op jit(solution)/shard_map/ppermute | solution.py:72
  334.2 12.1 %all-to-all-start.5 = ((f32[16,12,128]{2,1,0:T(8,128)}), f32[16,12,128]{2,1,0:T(8,128)S(1)}, u32[]{:S(2)}, u32[]{:S(2)}) async-start(f32[16,12,128]{2,1,0:T(8,128)} %reshape.311), calls=%async_computation.6 | async-start | bytes 262144 | tf_op jit(solution)/shard_map/all_to_all | solution.py:62
  375.3 10.1 %all-to-all-start.6 = ((f32[8,12,128]{2,1,0:T(8,128)}), f32[8,12,128]{2,1,0:T(8,128)S(1)}, u32[]{:S(2)}, u32[]{:S(2)}) async-start(f32[8,12,128]{2,1,0:T(8,128)} %broadcast_in_dim.16), calls=%async_computation.8 | async-start | bytes 131072 | tf_op jit(solution)/shard_map/all_to_all | solution.py:58
  381.1 21.7 %collective-permute-start.45 = (bf16[256,512]{1,0:T(8,128)(2,1)S(1)}, bf16[256,512]{1,0:T(8,128)(2,1)S(1)}, u32[]{:S(2)}, u32[]{:S(2)}) collective-permute-start(bf16[256,512]{1,0:T(8,128)(2,1)S(1)} %get-tuple-element.129), channel_id=1, source_target_pairs={{0,12},{4,0},{8,4},{12,8},{1,13},{5,1},{9,5},{13,9},{2,14},{6,2},{... | collective-permute-start | bytes 786440 | tf_op jit(solution)/shard_map/ppermute | solution.py:72
  383.6 19.2 %collective-permute-start.46 = (bf16[256,512]{1,0:T(8,128)(2,1)S(1)}, bf16[256,512]{1,0:T(8,128)(2,1)S(1)}, u32[]{:S(2)}, u32[]{:S(2)}) collective-permute-start(bf16[256,512]{1,0:T(8,128)(2,1)S(1)} %get-tuple-element.131), channel_id=1, source_target_pairs={{0,4},{4,8},{8,12},{12,0},{1,5},{5,9},{9,13},{13,1},{2,6},{6,10},{... | collective-permute-start | bytes 786440 | tf_op jit(solution)/shard_map/ppermute | solution.py:72
  383.6 19.2 %collective-permute-start.47 = (bf16[256,512]{1,0:T(8,128)(2,1)S(1)}, bf16[256,512]{1,0:T(8,128)(2,1)S(1)}, u32[]{:S(2)}, u32[]{:S(2)}) collective-permute-start(bf16[256,512]{1,0:T(8,128)(2,1)S(1)} %get-tuple-element.130), channel_id=1, source_target_pairs={{0,8},{4,12},{8,0},{12,4},{1,9},{5,13},{9,1},{13,5},{2,10},{6,14},... | collective-permute-start | bytes 786440 | tf_op jit(solution)/shard_map/ppermute | solution.py:72
  386.0 15.5 %all-to-all-start.7 = ((f32[16,12,128]{2,1,0:T(8,128)}), f32[16,12,128]{2,1,0:T(8,128)S(1)}, u32[]{:S(2)}, u32[]{:S(2)}) async-start(f32[16,12,128]{2,1,0:T(8,128)} %broadcast_in_dim.17), calls=%async_computation.9 | async-start | bytes 262144 | tf_op jit(solution)/shard_map/all_to_all | solution.py:58
  (30 other events, 174.7 us)
Sparse Core Ops, SparseCore 0:
  10.9 59.0 all-gather.3
  71.7 86.7 all-gather.5
  210.1 110.1 reduce-scatter.2
  322.5 52.0 reduce-scatter.4
